TPU v7x, 512 devices: a whole 4x4x16 slice. The times are simulated.
512 devices in a mesh: seq: 64 (over y_hi, z, core), tp: 8 (over y_lo, x).
Axes of the slice: x: 4, y: 4 (y_hi: 2, y_lo: 2; y = y_hi * 2 + y_lo), z: 16, core: 2. Of those that a mesh axis runs over, the one named last changes fastest.
Arguments:
- queries: bfloat16 [32768, 4096], P('seq', 'tp'), may hold values from -3 to 3
- keys: bfloat16 [32768, 4096], P('seq', 'tp'), may hold values from -3 to 3
- values: bfloat16 [32768, 4096], P('seq', 'tp'), may hold values from -6 to 6
- out_grad: bfloat16 [32768, 4096], P('seq', 'tp'), may hold values from -6 to 6
- gain: float32 [4096], P('tp'), may hold values from 0.5 to 1.5
- log_decay: float32 [32768, 32], P('seq', 'tp'), may hold values from -1 to 0, as said below
Outputs:
- query_grad: bfloat16 [32768, 4096], P('seq', 'tp')
- key_grad: bfloat16 [32768, 4096], P('seq', 'tp')
- value_grad: bfloat16 [32768, 4096], P('seq', 'tp')
- gain_grad: float32 [4096], P(('tp', 'seq'))
Inputs may be any that keep to these rules, and one draw needn't show every extreme that they name: `log_decay`: every entry is negative.
All inputs are finite; a program needn't handle non-finite values.
Results may differ from a plain program's by a relative error of at most 0.02.
Values may be sent and summed in bfloat16 or wider, within the bound.
No kernel may reach another device: no remote copies, remote signals or barrier semaphores. Data moves between devices by JAX's collectives and lax.ppermute only.
A program may use at most 64 MiB of HBM per device.

v0:
```python
import jax
import jax.numpy as jnp
from jax import lax
from jax.sharding import PartitionSpec as P

HEAD_GROUP = 32
HD = 128


def carried_in(value, axis, combine, identity, reverse):
    count, here = (lax.axis_size(axis), lax.axis_index(axis))
    everything = jax.tree.map(lambda part: lax.all_gather(part, axis), value)
    start = jax.tree.map(
        lambda part, zero: jnp.broadcast_to(jnp.asarray(zero, part.dtype), part.shape),
        value,
        identity,
    )

    def hop(k, before):
        at = count - 1 - k if reverse else k
        reached = at > here if reverse else at < here
        new = combine(before, jax.tree.map(lambda part: part[at], everything))
        return jax.tree.map(lambda a, b: jnp.where(reached, a, b), new, before)

    return lax.fori_loop(0, count, hop, start)


def decay_table(cumulative):
    length = cumulative.shape[0]
    row_index = jnp.arange(length)[:, None]
    col_index = jnp.arange(length)[None, :]
    causal = (row_index >= col_index)[None]
    spread_logs = cumulative.T[:, :, None] - cumulative.T[:, None, :]
    return jnp.where(causal, jnp.exp(jnp.where(causal, spread_logs, 0.0)), 0.0)


def chain_combine(earlier_item, later_item):
    return (
        earlier_item[0] * later_item[0],
        later_item[0][:, None, None] * earlier_item[1] + later_item[1],
    )


def shards(queries, keys, values, out_grad, gain, log_decay):
    length = queries.shape[0]
    heads_here = queries.shape[1] // HD
    shaped = (length, heads_here, HD)
    query_rows = queries.reshape(shaped)
    key_rows = keys.reshape(shaped)
    value_rows = values.reshape(shaped)
    cumulative = jnp.cumsum(log_decay, axis=0)
    block_total = cumulative[-1]
    weights = decay_table(cumulative)
    exp_cum = jnp.exp(cumulative)[:, :, None]
    exp_rest = jnp.exp(block_total[None] - cumulative)[:, :, None]
    scores = jnp.einsum("thd,shd->hts", query_rows, key_rows, preferred_element_type=jnp.float32)
    score_weights = (weights * scores).astype(jnp.bfloat16)
    scaled_keys = (key_rows * exp_rest).astype(jnp.bfloat16)
    update = jnp.einsum(
        "thd,the->hde", scaled_keys, value_rows, preferred_element_type=jnp.float32
    ).astype(jnp.bfloat16)
    unit_decay = jnp.ones((heads_here,), jnp.float32)
    empty_state = jnp.zeros((heads_here, HD, HD), jnp.float32)
    unused, carried_state = carried_in(
        (jnp.exp(block_total), update.astype(jnp.float32)),
        "seq",
        chain_combine,
        (unit_decay, empty_state),
        False,
    )
    state_half = carried_state.astype(jnp.bfloat16)
    inner_part = jnp.einsum(
        "hts,she->the", score_weights, value_rows, preferred_element_type=jnp.float32
    )
    carried = exp_cum * jnp.einsum(
        "thd,hde->the", query_rows, state_half, preferred_element_type=jnp.float32
    )
    attention = (inner_part + carried).reshape(length, heads_here * HD)
    upstream = gain[None] * out_grad.astype(jnp.float32)
    square_sum, dot_sum = lax.psum(
        (jnp.sum(attention * attention, axis=1), jnp.sum(attention * upstream, axis=1)), "tp"
    )
    feature_count = HEAD_GROUP * HD
    inverse = lax.rsqrt(square_sum / feature_count + 1e-05)
    mean_dot = dot_sum / feature_count
    attn_grad = (
        inverse[:, None] * upstream - (inverse * inverse * inverse * mean_dot)[:, None] * attention
    ).astype(jnp.bfloat16)
    gain_part = jnp.sum(out_grad.astype(jnp.float32) * attention * inverse[:, None], axis=0)
    gain_grad = lax.psum_scatter(gain_part, "seq", scatter_dimension=0, tiled=True)
    grad_rows = attn_grad.reshape(shaped)
    scaled_queries = (query_rows * exp_cum).astype(jnp.bfloat16)
    back_update = jnp.einsum(
        "thd,the->hde", scaled_queries, grad_rows, preferred_element_type=jnp.float32
    ).astype(jnp.bfloat16)
    unused_back, back_state = carried_in(
        (jnp.exp(block_total), back_update.astype(jnp.float32)),
        "seq",
        chain_combine,
        (unit_decay, empty_state),
        True,
    )
    back_half = back_state.astype(jnp.bfloat16)
    grad_scores = jnp.einsum(
        "the,she->hts", grad_rows, value_rows, preferred_element_type=jnp.float32
    )
    grad_mix = (weights * grad_scores).astype(jnp.bfloat16)
    query_grad = jnp.einsum(
        "hts,shd->thd", grad_mix, key_rows, preferred_element_type=jnp.float32
    ) + exp_cum * jnp.einsum(
        "the,hde->thd", grad_rows, state_half, preferred_element_type=jnp.float32
    )
    key_grad = jnp.einsum(
        "hts,thd->shd", grad_mix, query_rows, preferred_element_type=jnp.float32
    ) + exp_rest * jnp.einsum(
        "hde,the->thd", back_half, value_rows, preferred_element_type=jnp.float32
    )
    value_grad = jnp.einsum(
        "hts,the->she", score_weights, grad_rows, preferred_element_type=jnp.float32
    ) + exp_rest * jnp.einsum(
        "hde,thd->the", back_half, key_rows, preferred_element_type=jnp.float32
    )
    flat = (length, heads_here * HD)
    return (
        query_grad.reshape(flat).astype(jnp.bfloat16),
        key_grad.reshape(flat).astype(jnp.bfloat16),
        value_grad.reshape(flat).astype(jnp.bfloat16),
        gain_grad,
    )


def solution(mesh):
    in_specs = (
        P("seq", "tp"),
        P("seq", "tp"),
        P("seq", "tp"),
        P("seq", "tp"),
        P("tp"),
        P("seq", "tp"),
    )
    out_specs = (P("seq", "tp"), P("seq", "tp"), P("seq", "tp"), P(("tp", "seq")))
    return jax.shard_map(shards, mesh=mesh, in_specs=in_specs, out_specs=out_specs, check_vma=False)
```

profile of v0, /device:TPU:1, one launch (start us, length us, event | category | flops | bytes accessed | tf_op | source)
XLA Modules:
  0.0 593.8 jit_solution(5776778735756970955)
XLA Ops:
  8.0 1.2 reduce-window.6
  9.9 1.3 copy.108
  12.3 1.3 copy.107
  13.5 84.3 %all-gather.2 = f32[64,1,4]{2,1,0:T(1,128)S(1)} all-gather(f32[1,1,4]{2,1,0:T(1,128)S(1)} %bitcast.148), channel_id=1, replica_groups=mesh['seq'=64,'tp'=8] {'seq'}, dimensions={0}, use_global_device_ids=true | all-gather | bytes 1040 | tf_op jit(solution)/shard_map/all_gather | solution.py:12
  98.6 1.4 multiply_convert_fusion.1
  100.1 1.3 copy-done.1
  102.3 110.7 %all-gather.6.cloned.1.call-done = f32[256,128,128]{2,1,0:T(8,128)} async-done(((f32[4,128,128]{2,1,0:T(8,128)}), f32[256,128,128]{2,1,0:T(8,128)}) %all-gather.6.cloned.1.call-update) | async-done | bytes 16777232 | tf_op jit(solution)/shard_map/all_gather | solution.py:12
  213.0 70.2 %while.30 = (s32[]{:T(128)}, f32[4,128,128]{2,1,0:T(8,128)S(1)}, s32[]{:T(128)}, f32[64,4]{1,0:T(8,128)S(1)}, f32[64,4,128,128]{3,2,1,0:T(8,128)}, /*index=5*/s32[]{:T(128)}, s32[]{:T(128)}) while((s32[]{:T(128)}, f32[4,128,128]{2,1,0:T(8,128)S(1)}, s32[]{:T(128)}, f32[64,4]{1,0:T(8,128)S(1)}, f32[64,4,128,128]{3,2,1,0:T(8,128)}, ...), condition=%wide.region_3.4_spmd.clone, body=%wide.region_2.3_spmd.clone.sunk | while | flops 262148 | bytes 786593 | solution.py:25
  215.2 1.1 fusion.58
  216.3 1.1 fusion.58
  283.6 14.9 %psum.14 = f32[512]{0:T(512)S(1)} all-reduce(f32[512]{0:T(512)S(1)} %get-tuple-element.316), channel_id=1, replica_groups=mesh['seq'=64,'tp'=8] {'tp'}, use_global_device_ids=true, to_apply=%region_5.6 | all-reduce | flops 512 | bytes 4096 | tf_op jit(solution)/shard_map/psum | solution.py:80
  298.9 1.5 fusion.21
  300.4 12.5 %psum.15 = f32[512]{0:T(512)S(1)} all-reduce(f32[512]{0:T(512)S(1)} %get-tuple-element.289), channel_id=1, replica_groups=mesh['seq'=64,'tp'=8] {'tp'}, use_global_device_ids=true, to_apply=%region_7.8 | all-reduce | flops 512 | bytes 4096 | tf_op jit(solution)/shard_map/psum | solution.py:80
  312.9 1.3 fusion.18
  315.4 1.3 dynamic-slice
  317.4 1.6 multiply_convert_fusion
  319.8 2.7 fusion.10
  322.5 2.0 copy.126
  324.6 136.8 %all-reduce = f32[512]{0:T(512)S(1)} all-reduce(f32[512]{0:T(512)S(1)} %get-tuple-element.288), channel_id=4, replica_groups=mesh['seq'=64,'tp'=8] {'seq'}, use_global_device_ids=true, to_apply=%region_11.12.clone | all-reduce | flops 512 | bytes 4096
  462.0 2.5 convolution_bitcast_fusion.1
  464.5 1.5 convolution_bitcast_fusion
  466.1 46.4 %all-gather.8.cloned.1.call-done = f32[256,128,128]{2,1,0:T(8,128)} async-done(((f32[4,128,128]{2,1,0:T(8,128)}), f32[256,128,128]{2,1,0:T(8,128)}) %all-gather.8.cloned.1.call-update) | async-done | bytes 16777232 | tf_op jit(solution)/shard_map/all_gather | solution.py:12
  512.5 70.6 %while.31 = (s32[]{:T(128)}, f32[4,128,128]{2,1,0:T(8,128)S(1)}, s32[]{:T(128)}, f32[64,4]{1,0:T(8,128)S(1)}, f32[64,4,128,128]{3,2,1,0:T(8,128)}, /*index=5*/s32[]{:T(128)}, s32[]{:T(128)}, s32[]{:T(128)}, s32[]{:T(128)}) while((s32[]{:T(128)}, f32[4,128,128]{2,1,0:T(8,128)S(1)}, s32[]{:T(128)}, f32[64,4]{1,0:T(8,128)S(1)}, ...), condition=%wide.region_9.10_spmd.clone, body=%wide.region_8.9_spmd.clone.sunk | while | flops 262152 | bytes 786655 | solution.py:25
  583.1 1.6 fusion.12
  (306 shorter events, 144.1 us)
Async XLA Ops:
  7.2 4.0 copy-start
  7.2 205.8 %all-gather.6.cloned.1.call-start = ((), (), s32[]{:S(2)}) async-start(), calls=%async_computation | async-start | bytes 17039360 | tf_op jit(solution)/shard_map/all_gather | solution.py:12
  11.2 89.0 %copy-start.7 = (bf16[512,512]{0,1:T(8,128)(2,1)}, bf16[512,512]{0,1:T(8,128)(2,1)S(1)}, u32[]{:S(2)}) copy-start(bf16[512,512]{0,1:T(8,128)(2,1)S(1)} %copy.108) | copy-start | bytes 1572868
  12.2 500.3 %all-gather.8.cloned.1.call-start = ((), (), s32[]{:S(2)}) async-start(), calls=%async_computation.1 | async-start | bytes 17039360 | tf_op jit(solution)/shard_map/all_gather | solution.py:12
  13.5 300.9 %copy-start.5 = (bf16[512,512]{0,1:T(8,128)(2,1)}, bf16[512,512]{0,1:T(8,128)(2,1)S(1)}, u32[]{:S(2)}) copy-start(bf16[512,512]{0,1:T(8,128)(2,1)S(1)} %copy.107) | copy-start | bytes 1572868
  97.9 0.7 copy-start.10
  100.1 1.4 copy-start.1
  213.0 85.9 %copy-start.12 = (f32[512]{0:T(512)S(1)}, f32[512]{0:T(512)}, u32[]{:S(2)}) copy-start(f32[512]{0:T(512)} %param.14) | copy-start | bytes 6148
  298.8 18.5 %copy-start.11 = (pred[512,512]{1,0:T(8,128)(4,1)S(1)}, pred[512,512]{1,0:T(8,128)(4,1)}, u32[]{:S(2)}) copy-start(pred[512,512]{1,0:T(8,128)(4,1)} %copy-done.10) | copy-start | bytes 786436
  314.4 3.0 copy-start.6
  317.4 1.6 copy-start.8
  319.0 3.5 copy-start.3
  319.0 143.0 %copy-start.2 = (bf16[4,512,512]{2,1,0:T(8,128)(2,1)S(1)}, bf16[4,512,512]{2,1,0:T(8,128)(2,1)}, u32[]{:S(2)}) copy-start(bf16[4,512,512]{2,1,0:T(8,128)(2,1)} %copy-done.1) | copy-start | bytes 6291460
  461.4 3.1 copy-start.4
  464.5 118.6 %copy-start.9 = (bf16[512,512]{0,1:T(8,128)(2,1)S(1)}, bf16[512,512]{0,1:T(8,128)(2,1)}, u32[]{:S(2)}) copy-start(bf16[512,512]{0,1:T(8,128)(2,1)} %copy-done.7) | copy-start | bytes 1572868
Sparse Core Ops, SparseCore 0:
  12.3 200.6 all-gather.5
  315.5 196.9 all-gather.7
where the time goes:
time: 598 us; the launch traced here: 594 us
  blocking collectives  249 us (42%)
  waiting for transfers between devices  157 us (26%)
  other arithmetic  140 us (23%)
  matrix products  15.7 us (3%)
  between operations  15 us (3%)
  local copies, waits for them, and re-layouts  13.4 us (2%)
    all_gather x2, waiting for transfers between devices, carried_in(): everything = jax.tree.map(lambda part: lax.all_gather(part, axis), value)  157 us
    unnamed x1, blocking collectives  137 us
    select_n x128, other arithmetic, hop(): return jax.tree.map(lambda a, b: jnp.where(reached, a, b), new, before)  135 us
    all_gather x1, blocking collectives, carried_in(): everything = jax.tree.map(lambda part: lax.all_gather(part, axis), value)  84.3 us
    psum x2, blocking collectives, shards(): lax.psum((jnp.sum(attention * attention, axis=1), jnp.sum(attention * ups...  27.4 us
  transfers between devices with their start and end apart: 2, of which 2 were waited for; matrix products, arithmetic and copies ran while one was open for 3% of the time, Pallas kernels for 0%

commit v1 on v0

v1 whole, which is shorter than its diff:
```python
import jax
import jax.numpy as jnp
from jax import lax
from jax.experimental import pallas as pl
from jax.experimental.pallas import tpu as pltpu
from jax.sharding import PartitionSpec as P

HEAD_GROUP = 32
HD = 128
SIDE = 8
PIECE = 64
MESSAGE = PIECE + 16
TILE = 128
BF16, F32 = jnp.bfloat16, jnp.float32

NEAR = [[g * SIDE + m for m in range(SIDE)] for g in range(SIDE)]
FAR = [[g * SIDE + m for g in range(SIDE)] for m in range(SIDE)]


def mm(a, b):
    return lax.dot_general(a, b, (((1,), (0,)), ((), ())), preferred_element_type=F32)


def mm_nt(a, b):
    return lax.dot_general(a, b, (((1,), (1,)), ((), ())), preferred_element_type=F32)


def mm_tn(a, b):
    return lax.dot_general(a, b, (((0,), (0,)), ((), ())), preferred_element_type=F32)


def split3(x):
    high = x.astype(BF16)
    rest = x - high.astype(F32)
    mid = rest.astype(BF16)
    low = (rest - mid.astype(F32)).astype(BF16)
    return high, mid, low


def head(ref, h):
    return ref[:, h * HD : (h + 1) * HD]


def iota(shape, dim):
    return lax.broadcasted_iota(jnp.int32, shape, dim)


def scalar_rows(total):
    high, mid, low = (part.astype(F32) for part in split3(total))
    rows = iota((16, HD), 0)
    out = jnp.where(rows == 0, high, jnp.where(rows == 1, mid, jnp.where(rows == 2, low, 0.0)))
    return out.astype(BF16)


def read_scalar_row(tile):
    wide = tile.astype(F32)
    return wide[0:1] + wide[1:2] + wide[2:3]


def cumulate(ld_ref, cum_ref, col_ref):
    heads, length = ld_ref.shape
    upper = (iota((length, length), 0) <= iota((length, length), 1)).astype(BF16)
    lower = (iota((length, length), 0) >= iota((length, length), 1)).astype(BF16)
    parts = split3(ld_ref[...])
    cum_ref[...] = mm(parts[0], upper) + mm(parts[1], upper) + mm(parts[2], upper)
    col_ref[...] = mm_nt(lower, parts[0]) + mm_nt(lower, parts[1]) + mm_nt(lower, parts[2])


def update_kernel(k_ref, v_ref, ld_ref, send_ref, cum_ref, col_ref):
    cumulate(ld_ref, cum_ref, col_ref)
    length = k_ref.shape[0]
    for h in range(ld_ref.shape[0]):
        col = col_ref[:, h : h + 1]
        total = col[length - 1 : length]
        scaled = (head(k_ref, h).astype(F32) * jnp.exp(total - col)).astype(BF16)
        update = mm_tn(scaled, head(v_ref, h)).astype(BF16)
        scalars = scalar_rows(jnp.broadcast_to(total, (1, HD)))
        for half in range(2):
            send_ref[2 * h + half, :PIECE] = update[half * PIECE : (half + 1) * PIECE]
            send_ref[2 * h + half, PIECE:] = scalars


def group_kernel(got_ref, send_ref, tot_ref):
    acc = jnp.zeros((PIECE, HD), F32)
    group_total = jnp.zeros((1, HD), F32)
    for m in range(SIDE):
        total = read_scalar_row(got_ref[m, PIECE:])
        tot_ref[m : m + 1] = total
        acc = jnp.exp(total) * acc + got_ref[m, :PIECE].astype(F32)
        group_total = group_total + total
    scalars = scalar_rows(group_total)
    acc = acc.astype(BF16)
    for g in range(SIDE):
        send_ref[g, :PIECE] = acc
        send_ref[g, PIECE:] = scalars


def spread_kernel(me_ref, got_ref, far_ref, tot_ref, send_ref, far_tot_ref):
    group = me_ref[0]
    state = jnp.zeros((PIECE, HD), F32)
    for g in range(SIDE):
        total = read_scalar_row(far_ref[g, PIECE:])
        far_tot_ref[g : g + 1] = total
        state = jnp.where(g < group, jnp.exp(total) * state + far_ref[g, :PIECE].astype(F32), state)
    for m in range(SIDE):
        send_ref[m] = state.astype(BF16)
        state = jnp.exp(tot_ref[m : m + 1]) * state + got_ref[m, :PIECE].astype(F32)


def back_group_kernel(got_ref, tot_ref, send_ref):
    acc = jnp.zeros((PIECE, HD), F32)
    gain = jnp.zeros((1, HD), F32)
    for m in reversed(range(SIDE)):
        acc = jnp.exp(tot_ref[m : m + 1]) * acc + got_ref[m, :PIECE].astype(F32)
        gain = gain + got_ref[m, PIECE:].astype(F32)[0:1]
    feature = iota((HD, HD), 0)
    lane = iota((HD, HD), 1)
    pick = ((feature % 8) == lane).astype(BF16)
    mine = ((iota((SIDE, HD), 1) % 64) // 8) == iota((SIDE, HD), 0)
    picked = sum(mm(jnp.where(mine, part.astype(F32), 0.0).astype(BF16), pick) for part in split3(gain))
    high, mid, low = (part.astype(F32) for part in split3(picked))
    rows = iota((16, HD), 0)
    acc = acc.astype(BF16)
    for g in range(SIDE):
        send_ref[g, :PIECE] = acc
        tile = jnp.where(
            rows == 0, high[g : g + 1], jnp.where(rows == 1, mid[g : g + 1], jnp.where(rows == 2, low[g : g + 1], 0.0))
        )
        send_ref[g, PIECE:] = tile.astype(BF16)


def back_spread_kernel(me_ref, got_ref, far_ref, tot_ref, far_tot_ref, send_ref, gain_ref):
    group = me_ref[0]
    state = jnp.zeros((PIECE, HD), F32)
    gain = jnp.zeros((1, HD), F32)
    for g in reversed(range(SIDE)):
        gain = gain + read_scalar_row(far_ref[g, PIECE:])
        state = jnp.where(
            g > group, jnp.exp(far_tot_ref[g : g + 1]) * state + far_ref[g, :PIECE].astype(F32), state
        )
    gain_ref[...] = gain
    for m in reversed(range(SIDE)):
        send_ref[m] = state.astype(BF16)
        state = jnp.exp(tot_ref[m : m + 1]) * state + got_ref[m, :PIECE].astype(F32)


def within_rows(col, row, i):
    wide = (i + 1) * TILE
    spread = jnp.exp(col[i * TILE : wide] - row[:, :wide])
    causal = iota((TILE, wide), 1) <= i * TILE + iota((TILE, wide), 0)
    return spread, causal


def attention_kernel(q_ref, k_ref, v_ref, og_ref, gain_ref, cum_ref, col_ref, state_ref, att_ref, sums_ref):
    length = q_ref.shape[0]
    squares = [jnp.zeros((TILE, HD), F32) for _ in range(length // TILE)]
    dots = [jnp.zeros((TILE, HD), F32) for _ in range(length // TILE)]
    for h in range(cum_ref.shape[0]):
        q, k, v = head(q_ref, h), head(k_ref, h), head(v_ref, h)
        col, row = col_ref[:, h : h + 1], cum_ref[h : h + 1]
        gain = gain_ref[:, h * HD : (h + 1) * HD]
        carried = jnp.exp(col) * mm(q, state_ref[h * HD : (h + 1) * HD])
        for i in range(length // TILE):
            here, wide = slice(i * TILE, (i + 1) * TILE), (i + 1) * TILE
            spread, causal = within_rows(col, row, i)
            mix = jnp.where(causal, spread * mm_nt(q[here], k[:wide]), 0.0).astype(BF16)
            att = mm(mix, v[:wide]) + carried[here]
            att_ref[here, h * HD : (h + 1) * HD] = att
            upstream = gain * og_ref[here, h * HD : (h + 1) * HD].astype(F32)
            squares[i] = squares[i] + att * att
            dots[i] = dots[i] + att * upstream
    lane = iota((TILE, HD), 1)
    packed = jnp.zeros((TILE, HD), F32)
    count = length // TILE
    for i in range(count):
        packed = jnp.where(lane == i, jnp.sum(squares[i], axis=1, keepdims=True), packed)
        packed = jnp.where(lane == count + i, jnp.sum(dots[i], axis=1, keepdims=True), packed)
    sums = jnp.transpose(packed)[:SIDE]
    for t in range(sums_ref.shape[0]):
        sums_ref[t] = sums


def gradient_kernel(sums_ref, att_ref, og_ref, gain_ref, q_ref, col_ref, grad_ref, send_ref):
    length, features = att_ref.shape
    count = length // TILE
    sums = sums_ref[0]
    for t in range(1, sums_ref.shape[0]):
        sums = sums + sums_ref[t]
    sums = sums / (HEAD_GROUP * HD)
    inverse = lax.rsqrt(sums[:count] + 1e-05)
    slope = inverse * inverse * inverse * sums[count:]
    columns = jnp.transpose(
        jnp.concatenate([inverse, slope, jnp.zeros((TILE - 2 * count, TILE), F32)], axis=0)
    )
    inverse = jnp.concatenate([columns[:, i : i + 1] for i in range(count)], axis=0)
    slope = jnp.concatenate([columns[:, count + i : count + i + 1] for i in range(count)], axis=0)
    gains = []
    for h in range(features // HD):
        att = head(att_ref, h)
        out_grad = head(og_ref, h).astype(F32)
        upstream = gain_ref[:, h * HD : (h + 1) * HD] * out_grad
        grad = (inverse * upstream - slope * att).astype(BF16)
        grad_ref[:, h * HD : (h + 1) * HD] = grad
        gains.append(jnp.sum(out_grad * att * inverse, axis=0, keepdims=True))
        scaled = (head(q_ref, h).astype(F32) * jnp.exp(col_ref[:, h : h + 1])).astype(BF16)
        update = mm_tn(scaled, grad).astype(BF16)
        for half in range(2):
            send_ref[2 * h + half, :PIECE] = update[half * PIECE : (half + 1) * PIECE]
    gain_part = jnp.concatenate(gains, axis=1)
    high, mid, low = (part.astype(F32) for part in split3(gain_part))
    mine = ((iota((SIDE, features), 1) // 8) % 8) == iota((SIDE, features), 0)
    feature, lane = iota((features, HD), 0), iota((features, HD), 1)
    place = (feature // 64) * 8 + feature % 8
    to_high = (place == lane).astype(BF16)
    to_low = (place + 64 == lane).astype(BF16)
    picked = mm(jnp.where(mine, high, 0.0).astype(BF16), to_high) + mm(
        jnp.where(mine, mid, 0.0).astype(BF16), to_low
    )
    rows = iota((16, HD), 0)
    for m in range(SIDE):
        send_ref[m, PIECE:] = jnp.where(rows == 0, picked[m : m + 1], 0.0).astype(BF16)


def final_kernel(
    q_ref, k_ref, v_ref, grad_ref, cum_ref, col_ref, state_ref, back_ref, qg_ref, kg_ref, vg_ref, kacc_ref, vacc_ref
):
    length = q_ref.shape[0]
    for h in range(cum_ref.shape[0]):
        lanes = slice(h * HD, (h + 1) * HD)
        q, k, v, grad = head(q_ref, h), head(k_ref, h), head(v_ref, h), head(grad_ref, h)
        state, back = state_ref[lanes], back_ref[lanes]
        col, row = col_ref[:, h : h + 1], cum_ref[h : h + 1]
        rest = jnp.exp(col[length - 1 : length] - col)
        kacc_ref[...] = rest * mm_nt(v, back)
        vacc_ref[...] = rest * mm(k, back)
        carried = jnp.exp(col) * mm_nt(grad, state)
        for i in range(length // TILE):
            here, wide = slice(i * TILE, (i + 1) * TILE), (i + 1) * TILE
            spread, causal = within_rows(col, row, i)
            spread = jnp.where(causal, spread, 0.0)
            mix = (spread * mm_nt(q[here], k[:wide])).astype(BF16)
            grad_mix = (spread * mm_nt(grad[here], v[:wide])).astype(BF16)
            qg_ref[here, lanes] = (mm(grad_mix, k[:wide]) + carried[here]).astype(BF16)
            kacc_ref[:wide] += mm_tn(grad_mix, q[here])
            vacc_ref[:wide] += mm_tn(mix, grad[here])
        kg_ref[:, lanes] = kacc_ref[...].astype(BF16)
        vg_ref[:, lanes] = vacc_ref[...].astype(BF16)


def call(kernel, outs, *args, scratch=(), smem=0, vmem=24, flops=0):
    specs = [pl.BlockSpec(memory_space=pltpu.SMEM)] * smem
    specs += [pl.BlockSpec(memory_space=pltpu.VMEM)] * (len(args) - smem)
    out_specs = [pl.BlockSpec(memory_space=pltpu.VMEM)] * len(outs)
    return pl.pallas_call(
        kernel,
        out_shape=[jax.ShapeDtypeStruct(shape, dtype) for shape, dtype in outs],
        in_specs=specs,
        out_specs=out_specs,
        scratch_shapes=list(scratch),
        compiler_params=pltpu.CompilerParams(vmem_limit_bytes=vmem * 1024 * 1024),
    )(*args)


def exchange(parts, groups):
    return lax.all_to_all(parts, "seq", 0, 0, tiled=True, axis_index_groups=groups)


def shards(queries, keys, values, out_grad, gain, log_decay):
    length, features = queries.shape
    heads = features // HD
    gain_row = gain.reshape(1, features)
    group = (lax.axis_index("seq") // SIDE).astype(jnp.int32).reshape(1)
    message = ((SIDE, MESSAGE, HD), BF16)
    piece = ((SIDE, PIECE, HD), BF16)
    scalars = ((SIDE, HD), F32)
    send, cum, col = call(
        update_kernel,
        [message, ((heads, length), F32), ((length, heads), F32)],
        keys, values, log_decay.T,
    )
    near = exchange(send, NEAR)
    send, totals = call(group_kernel, [message, scalars], near)
    far = exchange(send, FAR)
    send, far_totals = call(spread_kernel, [piece, scalars], group, near, far, totals, smem=1)
    state = exchange(send, NEAR).reshape(features, HD)
    attention, sums = call(
        attention_kernel,
        [((length, features), F32), ((8, SIDE, HD), F32)],
        queries, keys, values, out_grad, gain_row, cum, col, state,
    )
    sums = lax.all_to_all(sums, "tp", 0, 0, tiled=True)
    grad, send = call(
        gradient_kernel,
        [((length, features), BF16), message],
        sums, attention, out_grad, gain_row, queries, col,
    )
    near = exchange(send, NEAR)
    (send,) = call(back_group_kernel, [message], near, totals)
    far = exchange(send, FAR)
    send, gain_grad = call(
        back_spread_kernel, [piece, ((1, HD), F32)], group, near, far, totals, far_totals, smem=1
    )
    back = exchange(send, NEAR).reshape(features, HD)
    flat = ((length, features), BF16)
    query_grad, key_grad, value_grad = call(
        final_kernel,
        [flat, flat, flat],
        queries, keys, values, grad, cum, col, state, back,
        scratch=[pltpu.VMEM((length, HD), F32)] * 2,
    )
    return query_grad, key_grad, value_grad, gain_grad[0, : features // (SIDE * SIDE)]


def solution(mesh):
    in_specs = (
        P("seq", "tp"),
        P("seq", "tp"),
        P("seq", "tp"),
        P("seq", "tp"),
        P("tp"),
        P("seq", "tp"),
    )
    out_specs = (P("seq", "tp"), P("seq", "tp"), P("seq", "tp"), P(("tp", "seq")))
    return jax.shard_map(shards, mesh=mesh, in_specs=in_specs, out_specs=out_specs, check_vma=False)
```

time: 598 us -> 125 us (0.21)
  blocking collectives: 249 us -> 66.2 us
  other arithmetic: 140 us -> 0 us
  waiting for transfers between devices: 157 us -> 19.8 us
  starting transfers between devices: 0.08 us -> 21.1 us
  matrix products: 15.7 us -> 0 us
  between operations: 15 us -> 0.68 us
  Pallas kernels: 0 us -> 13 us
  local copies, waits for them, and re-layouts: 13.4 us -> 3.96 us
    all_gather x2 -> x0, waiting for transfers between devices: 157 us -> none  [carried_in(): everything = jax.tree.map(lambda part: lax.all_gather(part, axis), value)]
    unnamed x1 -> x0, blocking collectives: 137 us -> none
    select_n x128 -> x0, other arithmetic: 135 us -> none  [hop(): return jax.tree.map(lambda a, b: jnp.where(reached, a, b), new, before)]
    all_gather x1 -> x0, blocking collectives: 84.3 us -> none  [carried_in(): everything = jax.tree.map(lambda part: lax.all_gather(part, axis), value)]
    all_to_all x0 -> x5, blocking collectives: none -> 66.2 us  [the longest x4 57.1 us: exchange(): lax.all_to_all(parts, 'seq', 0, 0, tiled=True, axis_index_groups=groups)]
    psum x2 -> x0, blocking collectives: 27.4 us -> none  [shards(): lax.psum((jnp.sum(attention * attention, axis=1), jnp.sum(attention * ups...]
    all_to_all x0 -> x2, starting transfers between devices: none -> 21.1 us  [exchange(): lax.all_to_all(parts, 'seq', 0, 0, tiled=True, axis_index_groups=groups)]
    all_to_all x0 -> x2, waiting for transfers between devices: none -> 19.8 us  [exchange(): lax.all_to_all(parts, 'seq', 0, 0, tiled=True, axis_index_groups=groups)]
  transfers between devices with their start and end apart: 2 -> 2, of which waited for: 2 -> 2; matrix products, arithmetic and copies ran while one was open for 3% -> 0% of each run, Pallas kernels for 0% -> 0%
where the time goes in v1:
time: 125 us
  blocking collectives  66.2 us (53%)
  starting transfers between devices  21.1 us (17%)
  waiting for transfers between devices  19.8 us (16%)
  Pallas kernels  13 us (10%)
  local copies, waits for them, and re-layouts  3.96 us (3%)
    all_to_all x4, blocking collectives, exchange(): lax.all_to_all(parts, 'seq', 0, 0, tiled=True, axis_index_groups=groups)  57.1 us
    all_to_all x2, starting transfers between devices, exchange(): lax.all_to_all(parts, 'seq', 0, 0, tiled=True, axis_index_groups=groups)  21.1 us
    all_to_all x2, waiting for transfers between devices, exchange(): lax.all_to_all(parts, 'seq', 0, 0, tiled=True, axis_index_groups=groups)  19.8 us
    pallas_call x8, Pallas kernels, call(): pl.pallas_call(kernel, out_shape=[jax.ShapeDtypeStruct(shape, dtype) for...  13 us
    all_to_all x1, blocking collectives, shards(): sums = lax.all_to_all(sums, 'tp', 0, 0, tiled=True)  9.04 us
    unnamed x16, local copies, waits for them, and re-layouts  3.45 us
  transfers between devices with their start and end apart: 2, of which 2 were waited for; matrix products, arithmetic and copies ran while one was open for 0% of the time, Pallas kernels for 0%

profile of v1, /device:TPU:1, one launch (start us, length us, event | category | flops | bytes accessed | tf_op | source)
XLA Modules:
  0.0 124.6 jit_solution(16738611717512681025)
XLA Ops:
  0.6 0.0 copy-start
  0.6 1.0 copy-done
  1.7 1.0 copy-done.2
  2.7 0.7 copy-done.6
  3.4 1.6 %shard_map.93 = (bf16[8,80,128]{2,1,0:T(8,128)(2,1)S(1)}, f32[4,512]{1,0:T(4,128)S(1)}, f32[512,4]{1,0:T(8,128)S(1)}) custom-call(bf16[512,512]{1,0:T(8,128)(2,1)S(1)} %copy-done, bf16[512,512]{1,0:T(8,128)(2,1)S(1)} %copy-done.2, f32[4,512]{1,0:T(4,128)S(1)} %bitcast.10), custom_call_target="tpu_custom_call" | custom-call | tf_op jit(solution)/shard_map/pallas_call | solution.py:254
  5.0 15.3 %all_to_all.35.got_ref = bf16[8,80,128]{2,1,0:T(8,128)(2,1)S(1)} all-to-all(bf16[8,80,128]{2,1,0:T(8,128)(2,1)S(1)} %get-tuple-element.22), channel_id=1, replica_groups={{0,8,16,24,32,40,48,56},{64,72,80,88,96,104,112,120},{128,136,144,152,1..., dimensions={0} | all-to-all | bytes 327680 | tf_op jit(solution)/shard_map/all_to_all | solution.py:265
  20.3 0.7 shard_map.94
  21.0 12.8 %all-to-all-start.1 = ((bf16[8,80,128]{2,1,0:T(8,128)(2,1)}), bf16[8,80,128]{2,1,0:T(8,128)(2,1)S(1)}, u32[]{:S(2)}, u32[]{:S(2)}) async-start(bf16[8,80,128]{2,1,0:T(8,128)(2,1)} %get-tuple-element.23), calls=%async_computation.1 | async-start | bytes 327680 | tf_op jit(solution)/shard_map/all_to_all | solution.py:265
  33.8 14.5 %all-to-all-done.1.far_ref = bf16[8,80,128]{2,1,0:T(8,128)(2,1)S(1)} async-done(((bf16[8,80,128]{2,1,0:T(8,128)(2,1)}), bf16[8,80,128]{2,1,0:T(8,128)(2,1)S(1)}, u32[]{:S(2)}, u32[]{:S(2)}) %all-to-all-start.1) | async-done | bytes 163872 | tf_op jit(solution)/shard_map/all_to_all | solution.py:265
  48.3 0.1 shard_map.95
  48.4 13.9 %all_to_all.36 = bf16[8,64,128]{2,1,0:T(8,128)(2,1)S(1)} all-to-all(bf16[8,64,128]{2,1,0:T(8,128)(2,1)S(1)} %get-tuple-element.25), channel_id=1, replica_groups={{0,8,16,24,32,40,48,56},{64,72,80,88,96,104,112,120},{128,136,144,152,1..., dimensions={0} | all-to-all | bytes 262144 | tf_op jit(solution)/shard_map/all_to_all | solution.py:265
  62.3 0.0 copy-done.4
  62.3 0.7 copy-done.7
  63.0 2.6 %shard_map.96 = (f32[512,512]{1,0:T(8,128)S(1)}, f32[8,8,128]{2,1,0:T(8,128)S(1)}) custom-call(bf16[512,512]{1,0:T(8,128)(2,1)S(1)} %copy-done.4, bf16[512,512]{1,0:T(8,128)(2,1)S(1)} %copy-done.1, bf16[512,512]{1,0:T(8,128)(2,1)S(1)} %copy-done.3, bf16[512,512]{1,0:T(8,128)(2,1)S(1)} %copy-done.5, f32[1,512]{1,0:T(1,128)S(1)} %bitcast.11, ...), custom_call_target="tpu_custom_call" | custom-call | tf_op jit(solution)/shard_map/pallas_call | solution.py:254
  65.6 9.0 %all_to_all.37.sums_ref = f32[8,8,128]{2,1,0:T(8,128)S(1)} all-to-all(f32[8,8,128]{2,1,0:T(8,128)S(1)} %get-tuple-element.26), channel_id=1, replica_groups=mesh['seq'=64,'tp'=8] {'tp'}, dimensions={0} | all-to-all | bytes 65536 | tf_op jit(solution)/shard_map/all_to_all | solution.py:291
  74.6 1.2 shard_map.97
  75.8 10.9 %all_to_all.38.got_ref = bf16[8,80,128]{2,1,0:T(8,128)(2,1)S(1)} all-to-all(bf16[8,80,128]{2,1,0:T(8,128)(2,1)S(1)} %get-tuple-element.29), channel_id=1, replica_groups={{0,8,16,24,32,40,48,56},{64,72,80,88,96,104,112,120},{128,136,144,152,1..., dimensions={0} | all-to-all | bytes 327680 | tf_op jit(solution)/shard_map/all_to_all | solution.py:265
  86.6 0.2 shard_map.98
  86.8 17.1 %all_to_all.39.far_ref = bf16[8,80,128]{2,1,0:T(8,128)(2,1)S(1)} all-to-all(bf16[8,80,128]{2,1,0:T(8,128)(2,1)S(1)} %shard_map.98), channel_id=1, replica_groups={{0,64,128,192,256,320,384,448},{8,72,136,200,264,328,392,456},{16,80,14..., dimensions={0} | all-to-all | bytes 327680 | tf_op jit(solution)/shard_map/all_to_all | solution.py:265
  103.9 0.7 shard_map.99
  104.6 8.3 %all-to-all-start.6 = ((bf16[8,64,128]{2,1,0:T(8,128)(2,1)}), bf16[8,64,128]{2,1,0:T(8,128)(2,1)S(1)}, u32[]{:S(2)}, u32[]{:S(2)}) async-start(bf16[8,64,128]{2,1,0:T(8,128)(2,1)} %get-tuple-element.31), calls=%async_computation.6 | async-start | bytes 262144 | tf_op jit(solution)/shard_map/all_to_all | solution.py:265
  112.9 0.5 slice_bitcast_fusion
  113.4 5.3 %all-to-all-done.6 = bf16[8,64,128]{2,1,0:T(8,128)(2,1)S(1)} async-done(((bf16[8,64,128]{2,1,0:T(8,128)(2,1)}), bf16[8,64,128]{2,1,0:T(8,128)(2,1)S(1)}, u32[]{:S(2)}, u32[]{:S(2)}) %all-to-all-start.6) | async-done | bytes 131104 | tf_op jit(solution)/shard_map/all_to_all | solution.py:265
  118.7 5.9 %shard_map.100 = (bf16[512,512]{1,0:T(8,128)(2,1)}, bf16[512,512]{1,0:T(8,128)(2,1)}, bf16[512,512]{1,0:T(8,128)(2,1)}) custom-call(bf16[512,512]{1,0:T(8,128)(2,1)S(1)} %copy-done.4, bf16[512,512]{1,0:T(8,128)(2,1)S(1)} %copy-done.1, bf16[512,512]{1,0:T(8,128)(2,1)S(1)} %copy-done.3, bf16[512,512]{1,0:T(8,128)(2,1)S(1)} %get-tuple-element.28.grad_ref, ...), custom_call_target="tpu_custom_call" | custom-call | tf_op jit(solution)/shard_map/pallas_call | solution.py:254
  (10 shorter events, 0.0 us)
Async XLA Ops:
  0.6 1.0 copy-start
  1.7 1.0 copy-start.2
  2.7 0.7 copy-start.6
  3.4 58.9 %copy-start.4 = (bf16[512,512]{1,0:T(8,128)(2,1)S(1)}, bf16[512,512]{1,0:T(8,128)(2,1)}, u32[]{:S(2)}) copy-start(bf16[512,512]{1,0:T(8,128)(2,1)} %q_ref.5) | copy-start | bytes 1572868
  3.4 58.9 %copy-start.5 = (bf16[512,512]{1,0:T(8,128)(2,1)S(1)}, bf16[512,512]{1,0:T(8,128)(2,1)}, u32[]{:S(2)}) copy-start(bf16[512,512]{1,0:T(8,128)(2,1)} %og_ref.3) | copy-start | bytes 1572868
  20.3 42.0 %copy-start.3 = (bf16[512,512]{1,0:T(8,128)(2,1)S(1)}, bf16[512,512]{1,0:T(8,128)(2,1)}, u32[]{:S(2)}) copy-start(bf16[512,512]{1,0:T(8,128)(2,1)} %v_ref.5) | copy-start | bytes 1572868
  21.0 41.3 %copy-start.1 = (bf16[512,512]{1,0:T(8,128)(2,1)S(1)}, bf16[512,512]{1,0:T(8,128)(2,1)}, u32[]{:S(2)}) copy-start(bf16[512,512]{1,0:T(8,128)(2,1)} %k_ref.5) | copy-start | bytes 1572868
  21.0 27.3 %all-to-all-start.1 = ((bf16[8,80,128]{2,1,0:T(8,128)(2,1)}), bf16[8,80,128]{2,1,0:T(8,128)(2,1)S(1)}, u32[]{:S(2)}, u32[]{:S(2)}) async-start(bf16[8,80,128]{2,1,0:T(8,128)(2,1)} %get-tuple-element.23), calls=%async_computation.1 | async-start | bytes 327680 | tf_op jit(solution)/shard_map/all_to_all | solution.py:265
  62.3 0.7 copy-start.7
  104.6 14.1 %all-to-all-start.6 = ((bf16[8,64,128]{2,1,0:T(8,128)(2,1)}), bf16[8,64,128]{2,1,0:T(8,128)(2,1)S(1)}, u32[]{:S(2)}, u32[]{:S(2)}) async-start(bf16[8,64,128]{2,1,0:T(8,128)(2,1)} %get-tuple-element.31), calls=%async_computation.6 | async-start | bytes 262144 | tf_op jit(solution)/shard_map/all_to_all | solution.py:265

commit v2 on v1

v2 whole, which is shorter than its diff:
```python
import jax
import jax.numpy as jnp
from jax import lax
from jax.experimental import pallas as pl
from jax.experimental.pallas import tpu as pltpu
from jax.sharding import PartitionSpec as P

HEAD_GROUP = 32
HD = 128
SIDE = 8
PIECE = 64
MESSAGE = PIECE + 8
TILE = 128
BLOCK = 256
HEAVY = 60 * 1024 * 1024
BF16, F32 = jnp.bfloat16, jnp.float32

NEAR = [[g * SIDE + m for m in range(SIDE)] for g in range(SIDE)]
FAR = [[g * SIDE + m for g in range(SIDE)] for m in range(SIDE)]


def mm(a, b):
    return lax.dot_general(a, b, (((1,), (0,)), ((), ())), preferred_element_type=F32)


def mm_nt(a, b):
    return lax.dot_general(a, b, (((1,), (1,)), ((), ())), preferred_element_type=F32)


def mm_tn(a, b):
    return lax.dot_general(a, b, (((0,), (0,)), ((), ())), preferred_element_type=F32)


def split3(x):
    high = x.astype(BF16)
    rest = x - high.astype(F32)
    mid = rest.astype(BF16)
    low = (rest - mid.astype(F32)).astype(BF16)
    return high, mid, low


def head(ref, h):
    return ref[:, h * HD : (h + 1) * HD]


def iota(shape, dim):
    return lax.broadcasted_iota(jnp.int32, shape, dim)


def rows_of(*parts):
    rows = iota((MESSAGE - PIECE, HD), 0)
    out = jnp.zeros((MESSAGE - PIECE, HD), F32)
    for n, part in enumerate(parts):
        out = jnp.where(rows == n, part.astype(F32), out)
    return out.astype(BF16)


def read_scalar_row(tile):
    wide = tile.astype(F32)
    return wide[0:1] + wide[1:2] + wide[2:3]


def stacked(ref):
    heads, length = ref.shape
    parts = [part.astype(F32) for part in split3(ref[...])]
    return jnp.concatenate(parts + [jnp.zeros((16 - 3 * heads, length), F32)], axis=0).astype(BF16)


def cumulative_columns(ld_ref):
    heads, length = ld_ref.shape
    lower = (iota((length, length), 0) >= iota((length, length), 1)).astype(BF16)
    sums = mm_nt(lower, stacked(ld_ref))
    return sums[:, :heads] + sums[:, heads : 2 * heads] + sums[:, 2 * heads : 3 * heads]


def cumulative_rows(ld_ref):
    heads, length = ld_ref.shape
    upper = (iota((length, length), 0) <= iota((length, length), 1)).astype(BF16)
    sums = mm(stacked(ld_ref), upper)
    return sums[:heads] + sums[heads : 2 * heads] + sums[2 * heads : 3 * heads]


def update_kernel(me_ref, k_hbm, v_hbm, ld_hbm, send_ref, place_ref, k_ref, v_ref, ld_ref, col_ref, sems, ld_sem):
    heads, length = ld_ref.shape
    ld_copy = pltpu.make_async_copy(ld_hbm, ld_ref, ld_sem)
    ld_copy.start()
    place_ref[...] = iota((SIDE, HD), 0) - me_ref[0]
    copies = []
    for n, (hbm, ref) in enumerate(((k_hbm, k_ref), (v_hbm, v_ref))):
        for i in range(length // TILE):
            rows = pl.ds(i * TILE, TILE)
            copies.append(pltpu.make_async_copy(hbm.at[rows], ref.at[rows], sems.at[n, i]))
            copies[-1].start()
    ld_copy.wait()
    col_ref[...] = cumulative_columns(ld_ref)
    for copy in copies:
        copy.wait()
    for h in range(heads):
        col = col_ref[:, h : h + 1]
        total = col[length - 1 : length]
        scaled = (head(k_ref, h).astype(F32) * jnp.exp(total - col)).astype(BF16)
        update = mm_tn(scaled, head(v_ref, h)).astype(BF16)
        scalars = rows_of(*split3(jnp.broadcast_to(total, (1, HD))))
        for half in range(2):
            send_ref[2 * h + half, :PIECE] = update[half * PIECE : (half + 1) * PIECE]
            send_ref[2 * h + half, PIECE:] = scalars


def group_kernel(got_ref, send_ref, tot_ref):
    acc = jnp.zeros((PIECE, HD), F32)
    group_total = jnp.zeros((1, HD), F32)
    for m in range(SIDE):
        total = read_scalar_row(got_ref[m, PIECE:])
        tot_ref[m : m + 1] = total
        acc = jnp.exp(total) * acc + got_ref[m, :PIECE].astype(F32)
        group_total = group_total + total
    scalars = rows_of(*split3(group_total))
    acc = acc.astype(BF16)
    for g in range(SIDE):
        send_ref[g, :PIECE] = acc
        send_ref[g, PIECE:] = scalars


def spread_kernel(got_ref, far_ref, tot_ref, place_ref, send_ref, far_tot_ref):
    state = jnp.zeros((PIECE, HD), F32)
    for g in range(SIDE):
        total = read_scalar_row(far_ref[g, PIECE:])
        far_tot_ref[g : g + 1] = total
        earlier = place_ref[g : g + 1] < 0
        state = jnp.where(earlier, jnp.exp(total) * state + far_ref[g, :PIECE].astype(F32), state)
    for m in range(SIDE):
        send_ref[m] = state.astype(BF16)
        state = jnp.exp(tot_ref[m : m + 1]) * state + got_ref[m, :PIECE].astype(F32)


def back_group_kernel(got_ref, tot_ref, send_ref):
    acc = jnp.zeros((PIECE, HD), F32)
    gain = jnp.zeros((1, HD), F32)
    for m in reversed(range(SIDE)):
        acc = jnp.exp(tot_ref[m : m + 1]) * acc + got_ref[m, :PIECE].astype(F32)
        gain = gain + got_ref[m, PIECE:].astype(F32)[0:1]
    feature = iota((HD, HD), 0)
    lane = iota((HD, HD), 1)
    pick = ((feature % 8) == lane).astype(BF16)
    mine = ((iota((SIDE, HD), 1) % 64) // 8) == iota((SIDE, HD), 0)
    picked = sum(mm(jnp.where(mine, part.astype(F32), 0.0).astype(BF16), pick) for part in split3(gain))
    parts = split3(picked)
    acc = acc.astype(BF16)
    for g in range(SIDE):
        send_ref[g, :PIECE] = acc
        send_ref[g, PIECE:] = rows_of(*(part[g : g + 1] for part in parts))


def back_spread_kernel(got_ref, far_ref, tot_ref, far_tot_ref, place_ref, send_ref, gain_ref):
    state = jnp.zeros((PIECE, HD), F32)
    gain = jnp.zeros((1, HD), F32)
    for g in reversed(range(SIDE)):
        gain = gain + read_scalar_row(far_ref[g, PIECE:])
        later = place_ref[g : g + 1] > 0
        state = jnp.where(later, jnp.exp(far_tot_ref[g : g + 1]) * state + far_ref[g, :PIECE].astype(F32), state)
    gain_ref[...] = gain
    for m in reversed(range(SIDE)):
        send_ref[m] = state.astype(BF16)
        state = jnp.exp(tot_ref[m : m + 1]) * state + got_ref[m, :PIECE].astype(F32)


def causal_tile():
    return iota((BLOCK, BLOCK), 1) <= iota((BLOCK, BLOCK), 0)


def decayed(scores, col, row, i, causal):
    here, start = slice(i * BLOCK, (i + 1) * BLOCK), i * BLOCK
    on = jnp.where(causal, jnp.exp(jnp.where(causal, col[here] - row[:, here], 0.0)), 0.0)
    if i == 0:
        return [(on * score).astype(BF16) for score in scores]
    base = row[:, start - 1 : start]
    off = jnp.exp(col[here] - base) * jnp.exp(base - row[:, :start])
    return [
        jnp.concatenate([(off * score[:, :start]).astype(BF16), (on * score[:, start:]).astype(BF16)], axis=1)
        for score in scores
    ]


def attention_kernel(
    q_ref, k_ref, v_ref, og_ref, gain_ref, ld_ref, state_ref, att_ref, sums_ref, mix_ref, row_ref, col_ref
):
    heads, length = ld_ref.shape
    count = length // TILE
    row_ref[...], col_ref[...] = cumulative_rows(ld_ref), cumulative_columns(ld_ref)
    grow = jnp.exp(col_ref[...])
    causal = causal_tile()
    squares = [jnp.zeros((BLOCK, HD), F32)] * (length // BLOCK)
    dots = [jnp.zeros((BLOCK, HD), F32)] * (length // BLOCK)
    for h in range(heads):
        lanes = slice(h * HD, (h + 1) * HD)
        q, k, v = head(q_ref, h), head(k_ref, h), head(v_ref, h)
        col, row = col_ref[:, h : h + 1], row_ref[h : h + 1]
        carried = grow[:, h : h + 1] * mm(q, state_ref[lanes])
        for i in range(length // BLOCK):
            here, wide = slice(i * BLOCK, (i + 1) * BLOCK), (i + 1) * BLOCK
            (mix,) = decayed([mm_nt(q[here], k[:wide])], col, row, i, causal)
            mix_ref[h, here, :wide] = mix
            att = mm(mix, v[:wide]) + carried[here]
            att_ref[here, lanes] = att
            squares[i] = squares[i] + att * att
            dots[i] = dots[i] + att * (gain_ref[:, lanes] * og_ref[here, lanes].astype(F32))
    squares, dots = jnp.concatenate(squares, axis=0), jnp.concatenate(dots, axis=0)
    lane = iota((TILE, HD), 1)
    packed = jnp.zeros((TILE, HD), F32)
    for i in range(count):
        here = slice(i * TILE, (i + 1) * TILE)
        packed = jnp.where(lane == i, jnp.sum(squares[here], axis=1, keepdims=True), packed)
        packed = jnp.where(lane == count + i, jnp.sum(dots[here], axis=1, keepdims=True), packed)
    sums = jnp.transpose(packed)[:SIDE]
    for t in range(sums_ref.shape[0]):
        sums_ref[t] = sums


def gradient_kernel(sums_ref, att_ref, og_ref, gain_ref, q_ref, col_ref, grad_ref, send_ref):
    length, features = att_ref.shape
    count = length // TILE
    sums = sums_ref[0]
    for t in range(1, sums_ref.shape[0]):
        sums = sums + sums_ref[t]
    sums = sums / (HEAD_GROUP * HD)
    inverse = lax.rsqrt(sums[:count] + 1e-05)
    slope = inverse * inverse * inverse * sums[count:]
    columns = jnp.transpose(
        jnp.concatenate([inverse, slope, jnp.zeros((TILE - 2 * count, TILE), F32)], axis=0)
    )
    inverse = jnp.concatenate([columns[:, i : i + 1] for i in range(count)], axis=0)
    slope = jnp.concatenate([columns[:, count + i : count + i + 1] for i in range(count)], axis=0)
    gains = []
    for h in range(features // HD):
        att = head(att_ref, h)
        out_grad = head(og_ref, h).astype(F32)
        upstream = gain_ref[:, h * HD : (h + 1) * HD] * out_grad
        grad = (inverse * upstream - slope * att).astype(BF16)
        grad_ref[:, h * HD : (h + 1) * HD] = grad
        gains.append(jnp.sum(out_grad * att * inverse, axis=0, keepdims=True))
        scaled = (head(q_ref, h).astype(F32) * jnp.exp(col_ref[:, h : h + 1])).astype(BF16)
        update = mm_tn(scaled, grad).astype(BF16)
        for half in range(2):
            send_ref[2 * h + half, :PIECE] = update[half * PIECE : (half + 1) * PIECE]
    gain_part = jnp.concatenate(gains, axis=1)
    high, mid, low = (part.astype(F32) for part in split3(gain_part))
    mine = ((iota((SIDE, features), 1) // 8) % 8) == iota((SIDE, features), 0)
    feature, lane = iota((features, HD), 0), iota((features, HD), 1)
    place = (feature // 64) * 8 + feature % 8
    to_high = (place == lane).astype(BF16)
    to_low = (place + 64 == lane).astype(BF16)
    picked = mm(jnp.where(mine, high, 0.0).astype(BF16), to_high) + mm(
        jnp.where(mine, mid, 0.0).astype(BF16), to_low
    )
    for m in range(SIDE):
        send_ref[m, PIECE:] = rows_of(picked[m : m + 1])


def final_kernel(
    q_ref, k_ref, v_ref, grad_ref, mix_ref, row_ref, col_ref, state_ref, back_ref, gain_row_ref,
    qg_hbm, kg_hbm, vg_hbm, gain_hbm,
    qg_ref, kg_ref, vg_ref, gain_ref, gmix_ref, sems, gain_sem,
):
    heads, length = row_ref.shape
    gain_ref[...] = gain_row_ref[0, : gain_ref.shape[0]]
    copies = [pltpu.make_async_copy(gain_ref, gain_hbm, gain_sem)]
    copies[0].start()
    causal = causal_tile()
    for h in range(heads):
        lanes = slice(h * HD, (h + 1) * HD)
        q, k, v, grad = head(q_ref, h), head(k_ref, h), head(v_ref, h), head(grad_ref, h)
        back = back_ref[lanes]
        col, row = col_ref[:, h : h + 1], row_ref[h : h + 1]
        rest = jnp.exp(col[length - 1 : length] - col)
        carried = jnp.exp(col) * mm_nt(grad, state_ref[lanes])
        for i in range(length // BLOCK):
            here, wide = slice(i * BLOCK, (i + 1) * BLOCK), (i + 1) * BLOCK
            (gmix,) = decayed([mm_nt(grad[here], v[:wide])], col, row, i, causal)
            gmix_ref[here, :wide] = gmix
            qg_ref[here, lanes] = (mm(gmix, k[:wide]) + carried[here]).astype(BF16)
        key_carried, value_carried = rest * mm_nt(v, back), rest * mm(k, back)
        for j in range(length // BLOCK):
            here, tail = slice(j * BLOCK, (j + 1) * BLOCK), slice(j * BLOCK, length)
            kg_ref[here, lanes] = (mm_tn(gmix_ref[tail, here], q[tail]) + key_carried[here]).astype(BF16)
            vg_ref[here, lanes] = (mm_tn(mix_ref[h, tail, here], grad[tail]) + value_carried[here]).astype(BF16)
        for n, (ref, hbm) in enumerate(((qg_ref, qg_hbm), (kg_ref, kg_hbm), (vg_ref, vg_hbm))):
            lanes = pl.ds(h * HD, HD)
            copies.append(pltpu.make_async_copy(ref.at[:, lanes], hbm.at[:, lanes], sems.at[n, h]))
            copies[-1].start()
    for copy in copies:
        copy.wait()


VMEM, SMEM, HBM = (pl.BlockSpec(memory_space=space) for space in (pltpu.VMEM, pltpu.SMEM, pltpu.HBM))


def call(kernel, outs, *args, ins=None, out_specs=None, scratch=(), vmem=16 * 1024 * 1024):
    return pl.pallas_call(
        kernel,
        out_shape=[jax.ShapeDtypeStruct(shape, dtype) for shape, dtype in outs],
        in_specs=ins or [VMEM] * len(args),
        out_specs=out_specs or [VMEM] * len(outs),
        scratch_shapes=list(scratch),
        compiler_params=pltpu.CompilerParams(vmem_limit_bytes=vmem),
    )(*args)


def exchange(parts, groups):
    return lax.all_to_all(parts, "seq", 0, 0, tiled=True, axis_index_groups=groups)


def shards(queries, keys, values, out_grad, gain, log_decay):
    length, features = queries.shape
    heads = features // HD
    gain_row = gain.reshape(1, features)
    decay_rows = log_decay.T
    group = (lax.axis_index("seq") // SIDE).astype(jnp.int32).reshape(1)
    message = ((SIDE, MESSAGE, HD), BF16)
    piece = ((SIDE, PIECE, HD), BF16)
    scalars = ((SIDE, HD), F32)
    half, whole, columns = ((length, features), BF16), ((length, features), F32), ((length, heads), F32)
    tiles = length // TILE
    place = ((SIDE, HD), jnp.int32)
    staging, dma = pltpu.VMEM(*half), pltpu.SemaphoreType.DMA
    send, place = call(
        update_kernel,
        [message, place],
        group, keys, values, decay_rows,
        ins=[SMEM, HBM, HBM, HBM],
        scratch=[staging, staging, pltpu.VMEM((heads, length), F32), pltpu.VMEM(*columns), dma((2, tiles)), dma],
        vmem=HEAVY,
    )
    near = exchange(send, NEAR)
    send, totals = call(group_kernel, [message, scalars], near)
    far = exchange(send, FAR)
    send, far_totals = call(spread_kernel, [piece, scalars], near, far, totals, place)
    state = exchange(send, NEAR).reshape(features, HD)
    cum_rows, mixes = ((heads, length), F32), ((heads, length, length), BF16)
    attention, sums, mix, row, col = call(
        attention_kernel,
        [whole, ((8, SIDE, HD), F32), mixes, cum_rows, columns],
        queries, keys, values, out_grad, gain_row, decay_rows, state,
    )
    sums = lax.all_to_all(sums, "tp", 0, 0, tiled=True)
    grad, send = call(
        gradient_kernel,
        [half, message],
        sums, attention, out_grad, gain_row, queries, col,
    )
    near = exchange(send, NEAR)
    (send,) = call(back_group_kernel, [message], near, totals)
    far = exchange(send, FAR)
    send, gain_grad = call(back_spread_kernel, [piece, ((1, HD), F32)], near, far, totals, far_totals, place)
    back = exchange(send, NEAR).reshape(features, HD)
    gain_out = ((features // (SIDE * SIDE),), F32)
    return call(
        final_kernel,
        [half, half, half, gain_out],
        queries, keys, values, grad, mix, row, col, state, back, gain_grad,
        out_specs=[HBM] * 4,
        scratch=[staging] * 3 + [pltpu.VMEM(*gain_out), pltpu.VMEM((length, length), BF16), dma((3, heads)), dma],
    )


def solution(mesh):
    in_specs = (
        P("seq", "tp"),
        P("seq", "tp"),
        P("seq", "tp"),
        P("seq", "tp"),
        P("tp"),
        P("seq", "tp"),
    )
    out_specs = (P("seq", "tp"), P("seq", "tp"), P("seq", "tp"), P(("tp", "seq")))
    return jax.shard_map(shards, mesh=mesh, in_specs=in_specs, out_specs=out_specs, check_vma=False)
```

time: 125 us -> 120 us (0.960)
  blocking collectives: 66.2 us -> 106 us
  starting transfers between devices: 21.1 us -> 0 us
  waiting for transfers between devices: 19.8 us -> 0 us
  local copies, waits for them, and re-layouts: 3.96 us -> 1.38 us
  Pallas kernels: 13 us -> 10.9 us
    all_to_all x4 -> x6, blocking collectives: 57.1 us -> 97.1 us  [exchange(): lax.all_to_all(parts, 'seq', 0, 0, tiled=True, axis_index_groups=groups)]
    all_to_all x2 -> x0, starting transfers between devices: 21.1 us -> none  [exchange(): lax.all_to_all(parts, 'seq', 0, 0, tiled=True, axis_index_groups=groups)]
    all_to_all x2 -> x0, waiting for transfers between devices: 19.8 us -> none  [exchange(): lax.all_to_all(parts, 'seq', 0, 0, tiled=True, axis_index_groups=groups)]
    pallas_call x8, Pallas kernels: 13 us -> 10.9 us  [call(): pl.pallas_call(kernel, out_shape=[jax.ShapeDtypeStruct(shape, dtype) for...]
    unnamed x16 -> x14, local copies, waits for them, and re-layouts: 3.45 us -> 1.38 us
  transfers between devices with their start and end apart: 2 -> 0, of which waited for: 2 -> 0; matrix products, arithmetic and copies ran while one was open for 0% -> 0% of each run, Pallas kernels for 0% -> 0%
where the time goes in v2:
time: 120 us; the launch traced here: 119 us
  blocking collectives  106 us (88%)
  Pallas kernels  10.9 us (9%)
  local copies, waits for them, and re-layouts  1.38 us (1%)
    all_to_all x6, blocking collectives, exchange(): lax.all_to_all(parts, 'seq', 0, 0, tiled=True, axis_index_groups=groups)  97.1 us
    pallas_call x8, Pallas kernels, call(): pl.pallas_call(kernel, out_shape=[jax.ShapeDtypeStruct(shape, dtype) for...  10.9 us
    all_to_all x1, blocking collectives, shards(): sums = lax.all_to_all(sums, 'tp', 0, 0, tiled=True)  9.04 us

profile of v2, /device:TPU:1, one launch (start us, length us, event | category | flops | bytes accessed | tf_op | source)
XLA Modules:
  0.0 119.2 jit_solution(4913869432755358139)
XLA Ops:
  0.6 0.0 copy-start.2
  0.6 0.0 copy-start.1
  0.7 0.0 copy-start.4
  0.7 0.0 copy-start
  0.7 0.0 copy-start.3
  0.7 3.3 %shard_map.93 = (bf16[8,72,128]{2,1,0:T(8,128)(2,1)}, s32[8,128]{1,0:T(8,128)}) custom-call(s32[1]{0:T(128)} %bitcast.2.me_ref, bf16[512,512]{1,0:T(8,128)(2,1)} %k_ref.3, bf16[512,512]{1,0:T(8,128)(2,1)} %v_ref.3, f32[4,512]{1,0:T(4,128)} %bitcast.8), custom_call_target="tpu_custom_call" | custom-call | tf_op jit(solution)/shard_map/pallas_call | solution.py:298
  4.0 16.1 %all_to_all.35.got_ref = bf16[8,72,128]{2,1,0:T(8,128)(2,1)S(1)} all-to-all(bf16[8,72,128]{2,1,0:T(8,128)(2,1)} %get-tuple-element.19), channel_id=1, replica_groups={{0,8,16,24,32,40,48,56},{64,72,80,88,96,104,112,120},{128,136,144,152,1..., dimensions={0} | all-to-all | bytes 294912 | tf_op jit(solution)/shard_map/all_to_all | solution.py:309
  20.1 26.3 %all_to_all.36.far_ref = bf16[8,72,128]{2,1,0:T(8,128)(2,1)S(1)} all-to-all(bf16[8,72,128]{2,1,0:T(8,128)(2,1)S(1)} %get-tuple-element.20), channel_id=1, replica_groups={{0,64,128,192,256,320,384,448},{8,72,136,200,264,328,392,456},{16,80,14..., dimensions={0} | all-to-all | bytes 294912 | tf_op jit(solution)/shard_map/all_to_all | solution.py:309
  46.4 0.7 copy-done.5
  47.1 0.1 shard_map.95
  47.2 13.2 %all_to_all.37 = bf16[8,64,128]{2,1,0:T(8,128)(2,1)S(1)} all-to-all(bf16[8,64,128]{2,1,0:T(8,128)(2,1)S(1)} %get-tuple-element.23), channel_id=1, replica_groups={{0,8,16,24,32,40,48,56},{64,72,80,88,96,104,112,120},{128,136,144,152,1..., dimensions={0} | all-to-all | bytes 262144 | tf_op jit(solution)/shard_map/all_to_all | solution.py:309
  60.4 0.0 copy-done.2
  60.4 0.0 copy-done.1
  60.4 0.0 copy-start.6
  60.4 0.7 copy-done.6
  61.1 2.3 %shard_map.96 = (f32[512,512]{1,0:T(8,128)S(1)}, f32[8,8,128]{2,1,0:T(8,128)S(1)}, bf16[4,512,512]{2,1,0:T(8,128)(2,1)S(1)}, f32[4,512]{1,0:T(4,128)S(1)}, f32[512,4]{1,0:T(8,128)S(1)}) custom-call(bf16[512,512]{1,0:T(8,128)(2,1)S(1)} %copy-done, bf16[512,512]{1,0:T(8,128)(2,1)S(1)} %copy-done.1, bf16[512,512]{1,0:T(8,128)(2,1)S(1)} %copy-done.2, ...), custom_call_target="tpu_custom_call" | custom-call | tf_op jit(solution)/shard_map/pallas_call | solution.py:298
  63.3 9.0 %all_to_all.38.sums_ref = f32[8,8,128]{2,1,0:T(8,128)S(1)} all-to-all(f32[8,8,128]{2,1,0:T(8,128)S(1)} %get-tuple-element.24), channel_id=1, replica_groups=mesh['seq'=64,'tp'=8] {'tp'}, dimensions={0} | all-to-all | bytes 65536 | tf_op jit(solution)/shard_map/all_to_all | solution.py:344
  72.4 1.3 %shard_map.97 = (bf16[512,512]{1,0:T(8,128)(2,1)S(1)}, bf16[8,72,128]{2,1,0:T(8,128)(2,1)S(1)}) custom-call(f32[8,8,128]{2,1,0:T(8,128)S(1)} %all_to_all.38.sums_ref, f32[512,512]{1,0:T(8,128)S(1)} %get-tuple-element.25.att_ref, bf16[512,512]{1,0:T(8,128)(2,1)S(1)} %copy-done.3, f32[1,512]{1,0:T(1,128)S(1)} %bitcast.11, bf16[512,512]{1,0:T(8,128)(2,1)S(1)} %copy-done, ...), custom_call_target="tpu_custom_call" | custom-call | tf_op jit(solution)/shard_map/pallas_call | solution.py:298
  73.6 10.8 %all_to_all.39.got_ref = bf16[8,72,128]{2,1,0:T(8,128)(2,1)S(1)} all-to-all(bf16[8,72,128]{2,1,0:T(8,128)(2,1)S(1)} %get-tuple-element.30), channel_id=1, replica_groups={{0,8,16,24,32,40,48,56},{64,72,80,88,96,104,112,120},{128,136,144,152,1..., dimensions={0} | all-to-all | bytes 294912 | tf_op jit(solution)/shard_map/all_to_all | solution.py:309
  84.4 0.2 shard_map.98
  84.6 17.8 %all_to_all.40.far_ref = bf16[8,72,128]{2,1,0:T(8,128)(2,1)S(1)} all-to-all(bf16[8,72,128]{2,1,0:T(8,128)(2,1)S(1)} %shard_map.98), channel_id=1, replica_groups={{0,64,128,192,256,320,384,448},{8,72,136,200,264,328,392,456},{16,80,14..., dimensions={0} | all-to-all | bytes 294912 | tf_op jit(solution)/shard_map/all_to_all | solution.py:309
  102.3 0.1 shard_map.99
  102.4 13.1 %all_to_all.41 = bf16[8,64,128]{2,1,0:T(8,128)(2,1)S(1)} all-to-all(bf16[8,64,128]{2,1,0:T(8,128)(2,1)S(1)} %get-tuple-element.32), channel_id=1, replica_groups={{0,8,16,24,32,40,48,56},{64,72,80,88,96,104,112,120},{128,136,144,152,1..., dimensions={0} | all-to-all | bytes 262144 | tf_op jit(solution)/shard_map/all_to_all | solution.py:309
  115.5 3.7 %shard_map.100 = (bf16[512,512]{1,0:T(8,128)(2,1)}, bf16[512,512]{1,0:T(8,128)(2,1)}, bf16[512,512]{1,0:T(8,128)(2,1)}, f32[8]{0:T(128)}) custom-call(bf16[512,512]{1,0:T(8,128)(2,1)S(1)} %copy-done, bf16[512,512]{1,0:T(8,128)(2,1)S(1)} %copy-done.1, bf16[512,512]{1,0:T(8,128)(2,1)S(1)} %copy-done.2, bf16[512,512]{1,0:T(8,128)(2,1)S(1)} %get-tuple-element.27.grad_ref, ...), custom_call_target="tpu_custom_call" | custom-call | tf_op jit(solution)/shard_map/pallas_call | solution.py:298
  (5 shorter events, 0.1 us)
Async XLA Ops:
  0.6 59.7 %copy-start.2 = (bf16[512,512]{1,0:T(8,128)(2,1)S(1)}, bf16[512,512]{1,0:T(8,128)(2,1)}, u32[]{:S(2)}) copy-start(bf16[512,512]{1,0:T(8,128)(2,1)} %v_ref.3) | copy-start | bytes 1572868
  0.6 59.7 %copy-start.1 = (bf16[512,512]{1,0:T(8,128)(2,1)S(1)}, bf16[512,512]{1,0:T(8,128)(2,1)}, u32[]{:S(2)}) copy-start(bf16[512,512]{1,0:T(8,128)(2,1)} %k_ref.3) | copy-start | bytes 1572868
  0.7 59.7 %copy-start.4 = (f32[512,4]{0,1:T(4,128)S(1)}, f32[512,4]{0,1:T(4,128)}, u32[]{:S(2)}) copy-start(f32[512,4]{0,1:T(4,128)} %param.11) | copy-start | bytes 24580
  0.7 59.7 %copy-start = (bf16[512,512]{1,0:T(8,128)(2,1)S(1)}, bf16[512,512]{1,0:T(8,128)(2,1)}, u32[]{:S(2)}) copy-start(bf16[512,512]{1,0:T(8,128)(2,1)} %q_ref.5) | copy-start | bytes 1572868
  0.7 59.7 %copy-start.3 = (bf16[512,512]{1,0:T(8,128)(2,1)S(1)}, bf16[512,512]{1,0:T(8,128)(2,1)}, u32[]{:S(2)}) copy-start(bf16[512,512]{1,0:T(8,128)(2,1)} %og_ref.3) | copy-start | bytes 1572868
  46.4 0.7 copy-start.5
  60.4 0.7 copy-start.6

commit v3 on v2

--- a/solution.py
+++ b/solution.py
@@ -12,7 +12,6 @@
 MESSAGE = PIECE + 8
 TILE = 128
 BLOCK = 256
-HEAVY = 60 * 1024 * 1024
 BF16, F32 = jnp.bfloat16, jnp.float32
 
 NEAR = [[g * SIDE + m for m in range(SIDE)] for g in range(SIDE)]
@@ -66,41 +65,46 @@
     return jnp.concatenate(parts + [jnp.zeros((16 - 3 * heads, length), F32)], axis=0).astype(BF16)
 
 
-def cumulative_columns(ld_ref):
-    heads, length = ld_ref.shape
-    lower = (iota((length, length), 0) >= iota((length, length), 1)).astype(BF16)
-    sums = mm_nt(lower, stacked(ld_ref))
-    return sums[:, :heads] + sums[:, heads : 2 * heads] + sums[:, 2 * heads : 3 * heads]
-
-
-def cumulative_rows(ld_ref):
+def cumulative(ld_ref):
     heads, length = ld_ref.shape
     upper = (iota((length, length), 0) <= iota((length, length), 1)).astype(BF16)
     sums = mm(stacked(ld_ref), upper)
-    return sums[:heads] + sums[heads : 2 * heads] + sums[2 * heads : 3 * heads]
-
-
-def update_kernel(me_ref, k_hbm, v_hbm, ld_hbm, send_ref, place_ref, k_ref, v_ref, ld_ref, col_ref, sems, ld_sem):
+    rows = sums[:heads] + sums[heads : 2 * heads] + sums[2 * heads : 3 * heads]
+    return rows, jnp.transpose(jnp.concatenate([rows, jnp.zeros((8 - heads, length), F32)], axis=0))
+
+
+def two_heads(ref, pair):
+    return ref[:, 2 * pair * HD : 2 * (pair + 1) * HD]
+
+
+def diagonal(ref, pair):
+    first, second = (ref[(2 * pair + n) * HD : (2 * pair + n + 1) * HD] for n in range(2))
+    zero = jnp.zeros_like(first)
+    return jnp.concatenate(
+        [jnp.concatenate([first, zero], axis=1), jnp.concatenate([zero, second], axis=1)], axis=0
+    )
+
+
+def update_kernel(me_ref, k_hbm, v_hbm, ld_hbm, send_ref, k_ref, v_ref, ld_ref, sems, ld_sem):
     heads, length = ld_ref.shape
     ld_copy = pltpu.make_async_copy(ld_hbm, ld_ref, ld_sem)
     ld_copy.start()
-    place_ref[...] = iota((SIDE, HD), 0) - me_ref[0]
     copies = []
-    for n, (hbm, ref) in enumerate(((k_hbm, k_ref), (v_hbm, v_ref))):
-        for i in range(length // TILE):
-            rows = pl.ds(i * TILE, TILE)
+    for i in range(length // TILE):
+        rows = pl.ds(i * TILE, TILE)
+        for n, (hbm, ref) in enumerate(((k_hbm, k_ref), (v_hbm, v_ref))):
             copies.append(pltpu.make_async_copy(hbm.at[rows], ref.at[rows], sems.at[n, i]))
             copies[-1].start()
     ld_copy.wait()
-    col_ref[...] = cumulative_columns(ld_ref)
+    unused, cols = cumulative(ld_ref)
+    total = cols[length - 1 : length]
+    rest = jnp.exp(total - cols)
     for copy in copies:
         copy.wait()
     for h in range(heads):
-        col = col_ref[:, h : h + 1]
-        total = col[length - 1 : length]
-        scaled = (head(k_ref, h).astype(F32) * jnp.exp(total - col)).astype(BF16)
+        scaled = (head(k_ref, h).astype(F32) * rest[:, h : h + 1]).astype(BF16)
         update = mm_tn(scaled, head(v_ref, h)).astype(BF16)
-        scalars = rows_of(*split3(jnp.broadcast_to(total, (1, HD))))
+        scalars = rows_of(*split3(jnp.broadcast_to(total[:, h : h + 1], (1, HD))))
         for half in range(2):
             send_ref[2 * h + half, :PIECE] = update[half * PIECE : (half + 1) * PIECE]
             send_ref[2 * h + half, PIECE:] = scalars
@@ -121,13 +125,13 @@
         send_ref[g, PIECE:] = scalars
 
 
-def spread_kernel(got_ref, far_ref, tot_ref, place_ref, send_ref, far_tot_ref):
+def spread_kernel(me_ref, got_ref, far_ref, tot_ref, send_ref, far_tot_ref):
+    group = me_ref[0]
     state = jnp.zeros((PIECE, HD), F32)
     for g in range(SIDE):
         total = read_scalar_row(far_ref[g, PIECE:])
         far_tot_ref[g : g + 1] = total
-        earlier = place_ref[g : g + 1] < 0
-        state = jnp.where(earlier, jnp.exp(total) * state + far_ref[g, :PIECE].astype(F32), state)
+        state = jnp.where(g < group, jnp.exp(total) * state + far_ref[g, :PIECE].astype(F32), state)
     for m in range(SIDE):
         send_ref[m] = state.astype(BF16)
         state = jnp.exp(tot_ref[m : m + 1]) * state + got_ref[m, :PIECE].astype(F32)
@@ -151,13 +155,13 @@
         send_ref[g, PIECE:] = rows_of(*(part[g : g + 1] for part in parts))
 
 
-def back_spread_kernel(got_ref, far_ref, tot_ref, far_tot_ref, place_ref, send_ref, gain_ref):
+def back_spread_kernel(me_ref, got_ref, far_ref, tot_ref, far_tot_ref, send_ref, gain_ref):
+    group = me_ref[0]
     state = jnp.zeros((PIECE, HD), F32)
     gain = jnp.zeros((1, HD), F32)
     for g in reversed(range(SIDE)):
         gain = gain + read_scalar_row(far_ref[g, PIECE:])
-        later = place_ref[g : g + 1] > 0
-        state = jnp.where(later, jnp.exp(far_tot_ref[g : g + 1]) * state + far_ref[g, :PIECE].astype(F32), state)
+        state = jnp.where(g > group, jnp.exp(far_tot_ref[g : g + 1]) * state + far_ref[g, :PIECE].astype(F32), state)
     gain_ref[...] = gain
     for m in reversed(range(SIDE)):
         send_ref[m] = state.astype(BF16)
@@ -182,29 +186,35 @@
 
 
 def attention_kernel(
-    q_ref, k_ref, v_ref, og_ref, gain_ref, ld_ref, state_ref, att_ref, sums_ref, mix_ref, row_ref, col_ref
+    q_ref, k_ref, v_ref, og_ref, gain_hbm, ld_ref, state_ref,
+    att_ref, sums_ref, mix_ref, row_ref, col_ref,
+    gain_ref, sem,
 ):
+    gain_copy = pltpu.make_async_copy(gain_hbm, gain_ref, sem)
+    gain_copy.start()
     heads, length = ld_ref.shape
     count = length // TILE
-    row_ref[...], col_ref[...] = cumulative_rows(ld_ref), cumulative_columns(ld_ref)
+    row_ref[...], col_ref[...] = cumulative(ld_ref)
     grow = jnp.exp(col_ref[...])
     causal = causal_tile()
-    squares = [jnp.zeros((BLOCK, HD), F32)] * (length // BLOCK)
-    dots = [jnp.zeros((BLOCK, HD), F32)] * (length // BLOCK)
+    carried = [mm(two_heads(q_ref, pair), diagonal(state_ref, pair)) for pair in range(heads // 2)]
     for h in range(heads):
         lanes = slice(h * HD, (h + 1) * HD)
         q, k, v = head(q_ref, h), head(k_ref, h), head(v_ref, h)
         col, row = col_ref[:, h : h + 1], row_ref[h : h + 1]
-        carried = grow[:, h : h + 1] * mm(q, state_ref[lanes])
+        own = grow[:, h : h + 1] * carried[h // 2][:, h % 2 * HD : (h % 2 + 1) * HD]
         for i in range(length // BLOCK):
             here, wide = slice(i * BLOCK, (i + 1) * BLOCK), (i + 1) * BLOCK
             (mix,) = decayed([mm_nt(q[here], k[:wide])], col, row, i, causal)
             mix_ref[h, here, :wide] = mix
-            att = mm(mix, v[:wide]) + carried[here]
-            att_ref[here, lanes] = att
-            squares[i] = squares[i] + att * att
-            dots[i] = dots[i] + att * (gain_ref[:, lanes] * og_ref[here, lanes].astype(F32))
-    squares, dots = jnp.concatenate(squares, axis=0), jnp.concatenate(dots, axis=0)
+            att_ref[here, lanes] = mm(mix, v[:wide]) + own[here]
+    gain_copy.wait()
+    squares, dots = jnp.zeros((length, HD), F32), jnp.zeros((length, HD), F32)
+    for h in range(heads):
+        lanes = slice(h * HD, (h + 1) * HD)
+        att = att_ref[:, lanes]
+        squares = squares + att * att
+        dots = dots + att * (gain_ref[:, lanes] * og_ref[:, lanes].astype(F32))
     lane = iota((TILE, HD), 1)
     packed = jnp.zeros((TILE, HD), F32)
     for i in range(count):
@@ -266,19 +276,24 @@
     copies = [pltpu.make_async_copy(gain_ref, gain_hbm, gain_sem)]
     copies[0].start()
     causal = causal_tile()
+    grow, rests = jnp.exp(col_ref[...]), jnp.exp(col_ref[length - 1 : length] - col_ref[...])
     for h in range(heads):
-        lanes = slice(h * HD, (h + 1) * HD)
+        if h % 2 == 0:
+            back = diagonal(back_ref, h // 2)
+            query_pair = mm_nt(two_heads(grad_ref, h // 2), diagonal(state_ref, h // 2))
+            key_pair = mm_nt(two_heads(v_ref, h // 2), back)
+            value_pair = mm(two_heads(k_ref, h // 2), back)
+        lanes, mine = slice(h * HD, (h + 1) * HD), slice(h % 2 * HD, (h % 2 + 1) * HD)
         q, k, v, grad = head(q_ref, h), head(k_ref, h), head(v_ref, h), head(grad_ref, h)
-        back = back_ref[lanes]
         col, row = col_ref[:, h : h + 1], row_ref[h : h + 1]
-        rest = jnp.exp(col[length - 1 : length] - col)
-        carried = jnp.exp(col) * mm_nt(grad, state_ref[lanes])
+        rest = rests[:, h : h + 1]
+        carried = grow[:, h : h + 1] * query_pair[:, mine]
         for i in range(length // BLOCK):
             here, wide = slice(i * BLOCK, (i + 1) * BLOCK), (i + 1) * BLOCK
             (gmix,) = decayed([mm_nt(grad[here], v[:wide])], col, row, i, causal)
             gmix_ref[here, :wide] = gmix
             qg_ref[here, lanes] = (mm(gmix, k[:wide]) + carried[here]).astype(BF16)
-        key_carried, value_carried = rest * mm_nt(v, back), rest * mm(k, back)
+        key_carried, value_carried = rest * key_pair[:, mine], rest * value_pair[:, mine]
         for j in range(length // BLOCK):
             here, tail = slice(j * BLOCK, (j + 1) * BLOCK), slice(j * BLOCK, length)
             kg_ref[here, lanes] = (mm_tn(gmix_ref[tail, here], q[tail]) + key_carried[here]).astype(BF16)
@@ -305,6 +320,10 @@
     )(*args)
 
 
+def in_hbm(*arrays):
+    return [pltpu.with_memory_space_constraint(x, pltpu.HBM) for x in arrays]
+
+
 def exchange(parts, groups):
     return lax.all_to_all(parts, "seq", 0, 0, tiled=True, axis_index_groups=groups)
 
@@ -318,28 +337,29 @@
     message = ((SIDE, MESSAGE, HD), BF16)
     piece = ((SIDE, PIECE, HD), BF16)
     scalars = ((SIDE, HD), F32)
-    half, whole, columns = ((length, features), BF16), ((length, features), F32), ((length, heads), F32)
-    tiles = length // TILE
-    place = ((SIDE, HD), jnp.int32)
+    half, whole, columns = ((length, features), BF16), ((length, features), F32), ((length, 8), F32)
     staging, dma = pltpu.VMEM(*half), pltpu.SemaphoreType.DMA
-    send, place = call(
+    (send,) = call(
         update_kernel,
-        [message, place],
-        group, keys, values, decay_rows,
+        [message],
+        group, *in_hbm(keys, values, decay_rows),
         ins=[SMEM, HBM, HBM, HBM],
-        scratch=[staging, staging, pltpu.VMEM((heads, length), F32), pltpu.VMEM(*columns), dma((2, tiles)), dma],
-        vmem=HEAVY,
+        scratch=[staging, staging, pltpu.VMEM((heads, length), F32), dma((2, length // TILE)), dma],
     )
     near = exchange(send, NEAR)
     send, totals = call(group_kernel, [message, scalars], near)
     far = exchange(send, FAR)
-    send, far_totals = call(spread_kernel, [piece, scalars], near, far, totals, place)
+    send, far_totals = call(
+        spread_kernel, [piece, scalars], group, near, far, totals, ins=[SMEM] + [VMEM] * 3
+    )
     state = exchange(send, NEAR).reshape(features, HD)
     cum_rows, mixes = ((heads, length), F32), ((heads, length, length), BF16)
     attention, sums, mix, row, col = call(
         attention_kernel,
         [whole, ((8, SIDE, HD), F32), mixes, cum_rows, columns],
         queries, keys, values, out_grad, gain_row, decay_rows, state,
+        ins=[VMEM] * 4 + [HBM] + [VMEM] * 2,
+        scratch=[pltpu.VMEM((1, features), F32), dma],
     )
     sums = lax.all_to_all(sums, "tp", 0, 0, tiled=True)
     grad, send = call(
@@ -350,7 +370,12 @@
     near = exchange(send, NEAR)
     (send,) = call(back_group_kernel, [message], near, totals)
     far = exchange(send, FAR)
-    send, gain_grad = call(back_spread_kernel, [piece, ((1, HD), F32)], near, far, totals, far_totals, place)
+    send, gain_grad = call(
+        back_spread_kernel,
+        [piece, ((1, HD), F32)],
+        group, near, far, totals, far_totals,
+        ins=[SMEM] + [VMEM] * 4,
+    )
     back = exchange(send, NEAR).reshape(features, HD)
     gain_out = ((features // (SIDE * SIDE),), F32)
     return call(

time: 120 us -> 116 us (0.967)
  local copies, waits for them, and re-layouts: 1.38 us -> 0.03 us
  Pallas kernels: 10.9 us -> 9.66 us
    unnamed x14 -> x12, local copies, waits for them, and re-layouts: 1.38 us -> 0.03 us
    pallas_call x8, Pallas kernels: 10.9 us -> 9.66 us  [call(): pl.pallas_call(kernel, out_shape=[jax.ShapeDtypeStruct(shape, dtype) for...]
where the time goes in v3:
time: 116 us
  blocking collectives  105 us (91%)
  Pallas kernels  9.66 us (8%)
    all_to_all x6, blocking collectives, exchange(): lax.all_to_all(parts, 'seq', 0, 0, tiled=True, axis_index_groups=groups)  96.3 us
    pallas_call x8, Pallas kernels, call(): pl.pallas_call(kernel, out_shape=[jax.ShapeDtypeStruct(shape, dtype) for...  9.66 us
    all_to_all x1, blocking collectives, shards(): sums = lax.all_to_all(sums, 'tp', 0, 0, tiled=True)  9.04 us

profile of v3, /device:TPU:1, one launch (start us, length us, event | category | flops | bytes accessed | tf_op | source)
XLA Modules:
  0.0 115.8 jit_solution(12355440318045627048)
XLA Ops:
  0.6 0.0 copy-start.1
  0.6 0.0 copy-start
  0.7 0.0 copy-start.4
  0.7 0.0 copy-start.2
  0.7 0.0 copy-start.3
  0.7 0.0 copy-start.5
  0.7 2.4 %shard_map.93 = bf16[8,72,128]{2,1,0:T(8,128)(2,1)S(1)} custom-call(s32[1]{0:T(128)} %bitcast.2.me_ref, bf16[512,512]{1,0:T(8,128)(2,1)} %k_ref.3, bf16[512,512]{1,0:T(8,128)(2,1)} %v_ref.3, f32[4,512]{1,0:T(4,128)} %bitcast.8), custom_call_target="tpu_custom_call" | custom-call | tf_op jit(solution)/shard_map/pallas_call | solution.py:313
  3.1 15.2 %all_to_all.35.got_ref = bf16[8,72,128]{2,1,0:T(8,128)(2,1)S(1)} all-to-all(bf16[8,72,128]{2,1,0:T(8,128)(2,1)S(1)} %shard_map.93), channel_id=1, replica_groups={{0,8,16,24,32,40,48,56},{64,72,80,88,96,104,112,120},{128,136,144,152,1..., dimensions={0} | all-to-all | bytes 294912 | tf_op jit(solution)/shard_map/all_to_all | solution.py:328
  18.3 27.0 %all_to_all.36.far_ref = bf16[8,72,128]{2,1,0:T(8,128)(2,1)S(1)} all-to-all(bf16[8,72,128]{2,1,0:T(8,128)(2,1)S(1)} %get-tuple-element.17), channel_id=1, replica_groups={{0,64,128,192,256,320,384,448},{8,72,136,200,264,328,392,456},{16,80,14..., dimensions={0} | all-to-all | bytes 294912 | tf_op jit(solution)/shard_map/all_to_all | solution.py:328
  45.3 0.1 shard_map.95
  45.4 13.1 %all_to_all.37 = bf16[8,64,128]{2,1,0:T(8,128)(2,1)S(1)} all-to-all(bf16[8,64,128]{2,1,0:T(8,128)(2,1)S(1)} %get-tuple-element.19), channel_id=1, replica_groups={{0,8,16,24,32,40,48,56},{64,72,80,88,96,104,112,120},{128,136,144,152,1..., dimensions={0} | all-to-all | bytes 262144 | tf_op jit(solution)/shard_map/all_to_all | solution.py:328
  58.5 0.0 copy-done.1
  58.5 0.0 copy-done.2
  58.5 0.0 copy-done.3
  58.5 0.0 copy-done.5
  58.5 2.1 %shard_map.96 = (f32[512,512]{1,0:T(8,128)S(1)}, f32[8,8,128]{2,1,0:T(8,128)S(1)}, bf16[4,512,512]{2,1,0:T(8,128)(2,1)S(1)}, f32[4,512]{1,0:T(4,128)S(1)}, f32[512,8]{1,0:T(8,128)S(1)}) custom-call(bf16[512,512]{1,0:T(8,128)(2,1)S(1)} %copy-done.2, bf16[512,512]{1,0:T(8,128)(2,1)S(1)} %copy-done, bf16[512,512]{1,0:T(8,128)(2,1)S(1)} %copy-done.1, ...), custom_call_target="tpu_custom_call" | custom-call | tf_op jit(solution)/shard_map/pallas_call | solution.py:313
  60.6 9.0 %all_to_all.38.sums_ref = f32[8,8,128]{2,1,0:T(8,128)S(1)} all-to-all(f32[8,8,128]{2,1,0:T(8,128)S(1)} %get-tuple-element.20), channel_id=1, replica_groups=mesh['seq'=64,'tp'=8] {'tp'}, dimensions={0} | all-to-all | bytes 65536 | tf_op jit(solution)/shard_map/all_to_all | solution.py:364
  69.6 1.3 %shard_map.97 = (bf16[512,512]{1,0:T(8,128)(2,1)S(1)}, bf16[8,72,128]{2,1,0:T(8,128)(2,1)S(1)}) custom-call(f32[8,8,128]{2,1,0:T(8,128)S(1)} %all_to_all.38.sums_ref, f32[512,512]{1,0:T(8,128)S(1)} %get-tuple-element.21.att_ref, bf16[512,512]{1,0:T(8,128)(2,1)S(1)} %copy-done.3, f32[1,512]{1,0:T(1,128)S(1)} %bitcast.11, bf16[512,512]{1,0:T(8,128)(2,1)S(1)} %copy-done.2, ...), custom_call_target="tpu_custom_call" | custom-call | tf_op jit(solution)/shard_map/pallas_call | solution.py:313
  70.9 10.8 %all_to_all.39.got_ref = bf16[8,72,128]{2,1,0:T(8,128)(2,1)S(1)} all-to-all(bf16[8,72,128]{2,1,0:T(8,128)(2,1)S(1)} %get-tuple-element.26), channel_id=1, replica_groups={{0,8,16,24,32,40,48,56},{64,72,80,88,96,104,112,120},{128,136,144,152,1..., dimensions={0} | all-to-all | bytes 294912 | tf_op jit(solution)/shard_map/all_to_all | solution.py:328
  81.7 0.2 shard_map.98
  81.9 17.2 %all_to_all.40.far_ref = bf16[8,72,128]{2,1,0:T(8,128)(2,1)S(1)} all-to-all(bf16[8,72,128]{2,1,0:T(8,128)(2,1)S(1)} %shard_map.98), channel_id=1, replica_groups={{0,64,128,192,256,320,384,448},{8,72,136,200,264,328,392,456},{16,80,14..., dimensions={0} | all-to-all | bytes 294912 | tf_op jit(solution)/shard_map/all_to_all | solution.py:328
  99.1 0.1 shard_map.99
  99.2 13.1 %all_to_all.41 = bf16[8,64,128]{2,1,0:T(8,128)(2,1)S(1)} all-to-all(bf16[8,64,128]{2,1,0:T(8,128)(2,1)S(1)} %get-tuple-element.28), channel_id=1, replica_groups={{0,8,16,24,32,40,48,56},{64,72,80,88,96,104,112,120},{128,136,144,152,1..., dimensions={0} | all-to-all | bytes 262144 | tf_op jit(solution)/shard_map/all_to_all | solution.py:328
  112.2 3.6 %shard_map.100 = (bf16[512,512]{1,0:T(8,128)(2,1)}, bf16[512,512]{1,0:T(8,128)(2,1)}, bf16[512,512]{1,0:T(8,128)(2,1)}, f32[8]{0:T(128)}) custom-call(bf16[512,512]{1,0:T(8,128)(2,1)S(1)} %copy-done.2, bf16[512,512]{1,0:T(8,128)(2,1)S(1)} %copy-done, bf16[512,512]{1,0:T(8,128)(2,1)S(1)} %copy-done.1, bf16[512,512]{1,0:T(8,128)(2,1)S(1)} %get-tuple-element.23.grad_ref, ...), custom_call_target="tpu_custom_call" | custom-call | tf_op jit(solution)/shard_map/pallas_call | solution.py:313
  (3 shorter events, 0.1 us)
Async XLA Ops:
  0.6 57.8 %copy-start.1 = (bf16[512,512]{1,0:T(8,128)(2,1)S(1)}, bf16[512,512]{1,0:T(8,128)(2,1)}, u32[]{:S(2)}) copy-start(bf16[512,512]{1,0:T(8,128)(2,1)} %v_ref.3) | copy-start | bytes 1572868
  0.6 57.8 %copy-start = (bf16[512,512]{1,0:T(8,128)(2,1)S(1)}, bf16[512,512]{1,0:T(8,128)(2,1)}, u32[]{:S(2)}) copy-start(bf16[512,512]{1,0:T(8,128)(2,1)} %k_ref.3) | copy-start | bytes 1572868
  0.7 57.8 %copy-start.4 = (f32[512,4]{0,1:T(4,128)S(1)}, f32[512,4]{0,1:T(4,128)}, u32[]{:S(2)}) copy-start(f32[512,4]{0,1:T(4,128)} %param.11) | copy-start | bytes 24580
  0.7 57.8 %copy-start.2 = (bf16[512,512]{1,0:T(8,128)(2,1)S(1)}, bf16[512,512]{1,0:T(8,128)(2,1)}, u32[]{:S(2)}) copy-start(bf16[512,512]{1,0:T(8,128)(2,1)} %q_ref.5) | copy-start | bytes 1572868
  0.7 57.8 %copy-start.3 = (bf16[512,512]{1,0:T(8,128)(2,1)S(1)}, bf16[512,512]{1,0:T(8,128)(2,1)}, u32[]{:S(2)}) copy-start(bf16[512,512]{1,0:T(8,128)(2,1)} %og_ref.3) | copy-start | bytes 1572868
  0.7 57.8 %copy-start.5 = (f32[512]{0:T(512)S(1)}, f32[512]{0:T(512)}, u32[]{:S(2)}) copy-start(f32[512]{0:T(512)} %param.10) | copy-start | bytes 6148

commit v4 on v3

--- a/solution.py
+++ b/solution.py
@@ -155,7 +155,7 @@
         send_ref[g, PIECE:] = rows_of(*(part[g : g + 1] for part in parts))
 
 
-def back_spread_kernel(me_ref, got_ref, far_ref, tot_ref, far_tot_ref, send_ref, gain_ref):
+def back_spread_kernel(me_ref, got_ref, far_ref, tot_ref, far_tot_ref, after_ref, send_ref, gain_ref):
     group = me_ref[0]
     state = jnp.zeros((PIECE, HD), F32)
     gain = jnp.zeros((1, HD), F32)
@@ -185,34 +185,47 @@
     ]
 
 
-def attention_kernel(
-    q_ref, k_ref, v_ref, og_ref, gain_hbm, ld_ref, state_ref,
-    att_ref, sums_ref, mix_ref, row_ref, col_ref,
-    gain_ref, sem,
+def inner_kernel(
+    q_hbm, k_hbm, v_hbm, gain_hbm, ld_ref, after_ref,
+    inner_ref, row_ref, col_ref, gain_ref,
+    q_ref, k_ref, v_ref, sems, gain_sem,
 ):
-    gain_copy = pltpu.make_async_copy(gain_hbm, gain_ref, sem)
+    heads, length = ld_ref.shape
+    gain_copy = pltpu.make_async_copy(gain_hbm, gain_ref, gain_sem)
     gain_copy.start()
-    heads, length = ld_ref.shape
-    count = length // TILE
+    copies = []
+    for pair in range(heads // 2):
+        lanes = pl.ds(2 * pair * HD, 2 * HD)
+        for n, (hbm, ref) in enumerate(((q_hbm, q_ref), (k_hbm, k_ref), (v_hbm, v_ref))):
+            copies.append(pltpu.make_async_copy(hbm.at[:, lanes], ref.at[:, lanes], sems.at[n, pair]))
+            copies[-1].start()
     row_ref[...], col_ref[...] = cumulative(ld_ref)
-    grow = jnp.exp(col_ref[...])
     causal = causal_tile()
-    carried = [mm(two_heads(q_ref, pair), diagonal(state_ref, pair)) for pair in range(heads // 2)]
     for h in range(heads):
-        lanes = slice(h * HD, (h + 1) * HD)
+        if h % 2 == 0:
+            for copy in copies[3 * (h // 2) : 3 * (h // 2 + 1)]:
+                copy.wait()
         q, k, v = head(q_ref, h), head(k_ref, h), head(v_ref, h)
         col, row = col_ref[:, h : h + 1], row_ref[h : h + 1]
-        own = grow[:, h : h + 1] * carried[h // 2][:, h % 2 * HD : (h % 2 + 1) * HD]
         for i in range(length // BLOCK):
             here, wide = slice(i * BLOCK, (i + 1) * BLOCK), (i + 1) * BLOCK
             (mix,) = decayed([mm_nt(q[here], k[:wide])], col, row, i, causal)
-            mix_ref[h, here, :wide] = mix
-            att_ref[here, lanes] = mm(mix, v[:wide]) + own[here]
+            inner_ref[here, h * HD : (h + 1) * HD] = mm(mix, v[:wide])
     gain_copy.wait()
+
+
+def attention_kernel(q_ref, og_ref, gain_ref, inner_ref, col_ref, state_ref, att_ref, sums_ref):
+    length, features = q_ref.shape
+    heads = features // HD
+    count = length // TILE
+    grow = jnp.exp(col_ref[...])
     squares, dots = jnp.zeros((length, HD), F32), jnp.zeros((length, HD), F32)
     for h in range(heads):
-        lanes = slice(h * HD, (h + 1) * HD)
-        att = att_ref[:, lanes]
+        lanes, mine = slice(h * HD, (h + 1) * HD), slice(h % 2 * HD, (h % 2 + 1) * HD)
+        if h % 2 == 0:
+            carried = mm(two_heads(q_ref, h // 2), diagonal(state_ref, h // 2))
+        att = inner_ref[:, lanes].astype(F32) + grow[:, h : h + 1] * carried[:, mine]
+        att_ref[:, lanes] = att
         squares = squares + att * att
         dots = dots + att * (gain_ref[:, lanes] * og_ref[:, lanes].astype(F32))
     lane = iota((TILE, HD), 1)
@@ -266,42 +279,69 @@
         send_ref[m, PIECE:] = rows_of(picked[m : m + 1])
 
 
-def final_kernel(
-    q_ref, k_ref, v_ref, grad_ref, mix_ref, row_ref, col_ref, state_ref, back_ref, gain_row_ref,
-    qg_hbm, kg_hbm, vg_hbm, gain_hbm,
-    qg_ref, kg_ref, vg_ref, gain_ref, gmix_ref, sems, gain_sem,
+def local_grad_kernel(
+    q_hbm, k_hbm, v_hbm, grad_ref, row_ref, col_ref, state_ref, after_ref,
+    qg_hbm, kacc_ref, vacc_ref,
+    q_ref, k_ref, v_ref, qg_ref, mix_ref, gmix_ref, sems, out_sems,
 ):
     heads, length = row_ref.shape
+    ins, outs = [], []
+    for pair in range(heads // 2):
+        lanes = pl.ds(2 * pair * HD, 2 * HD)
+        for n, (hbm, ref) in enumerate(((v_hbm, v_ref), (k_hbm, k_ref), (q_hbm, q_ref))):
+            ins.append(pltpu.make_async_copy(hbm.at[:, lanes], ref.at[:, lanes], sems.at[n, pair]))
+            ins[-1].start()
+    causal = causal_tile()
+    grow = jnp.exp(col_ref[...])
+    for h in range(heads):
+        if h % 2 == 0:
+            query_pair = mm_nt(two_heads(grad_ref, h // 2), diagonal(state_ref, h // 2))
+            for copy in ins[3 * (h // 2) : 3 * (h // 2 + 1)]:
+                copy.wait()
+        lanes, mine = slice(h * HD, (h + 1) * HD), slice(h % 2 * HD, (h % 2 + 1) * HD)
+        q, k, v, grad = head(q_ref, h), head(k_ref, h), head(v_ref, h), head(grad_ref, h)
+        col, row = col_ref[:, h : h + 1], row_ref[h : h + 1]
+        carried = grow[:, h : h + 1] * query_pair[:, mine]
+        for i in range(length // BLOCK):
+            here, wide = slice(i * BLOCK, (i + 1) * BLOCK), (i + 1) * BLOCK
+            gmix, mix = decayed([mm_nt(grad[here], v[:wide]), mm_nt(q[here], k[:wide])], col, row, i, causal)
+            mix_ref[here, :wide] = mix
+            gmix_ref[here, :wide] = gmix
+            qg_ref[here, lanes] = (mm(gmix, k[:wide]) + carried[here]).astype(BF16)
+        for j in range(length // BLOCK):
+            here, tail = slice(j * BLOCK, (j + 1) * BLOCK), slice(j * BLOCK, length)
+            kacc_ref[here, lanes] = mm_tn(gmix_ref[tail, here], q[tail]).astype(BF16)
+            vacc_ref[here, lanes] = mm_tn(mix_ref[tail, here], grad[tail]).astype(BF16)
+        lanes = pl.ds(h * HD, HD)
+        outs.append(pltpu.make_async_copy(qg_ref.at[:, lanes], qg_hbm.at[:, lanes], out_sems.at[h]))
+        outs[-1].start()
+    for copy in outs:
+        copy.wait()
+
+
+def final_kernel(
+    k_ref, v_ref, col_ref, back_ref, kacc_ref, vacc_ref, gain_row_ref,
+    kg_hbm, vg_hbm, gain_hbm,
+    kg_ref, vg_ref, gain_ref, sems, gain_sem,
+):
+    length = col_ref.shape[0]
     gain_ref[...] = gain_row_ref[0, : gain_ref.shape[0]]
     copies = [pltpu.make_async_copy(gain_ref, gain_hbm, gain_sem)]
     copies[0].start()
-    causal = causal_tile()
-    grow, rests = jnp.exp(col_ref[...]), jnp.exp(col_ref[length - 1 : length] - col_ref[...])
-    for h in range(heads):
-        if h % 2 == 0:
-            back = diagonal(back_ref, h // 2)
-            query_pair = mm_nt(two_heads(grad_ref, h // 2), diagonal(state_ref, h // 2))
-            key_pair = mm_nt(two_heads(v_ref, h // 2), back)
-            value_pair = mm(two_heads(k_ref, h // 2), back)
-        lanes, mine = slice(h * HD, (h + 1) * HD), slice(h % 2 * HD, (h % 2 + 1) * HD)
-        q, k, v, grad = head(q_ref, h), head(k_ref, h), head(v_ref, h), head(grad_ref, h)
-        col, row = col_ref[:, h : h + 1], row_ref[h : h + 1]
-        rest = rests[:, h : h + 1]
-        carried = grow[:, h : h + 1] * query_pair[:, mine]
-        for i in range(length // BLOCK):
-            here, wide = slice(i * BLOCK, (i + 1) * BLOCK), (i + 1) * BLOCK
-            (gmix,) = decayed([mm_nt(grad[here], v[:wide])], col, row, i, causal)
-            gmix_ref[here, :wide] = gmix
-            qg_ref[here, lanes] = (mm(gmix, k[:wide]) + carried[here]).astype(BF16)
-        key_carried, value_carried = rest * key_pair[:, mine], rest * value_pair[:, mine]
-        for j in range(length // BLOCK):
-            here, tail = slice(j * BLOCK, (j + 1) * BLOCK), slice(j * BLOCK, length)
-            kg_ref[here, lanes] = (mm_tn(gmix_ref[tail, here], q[tail]) + key_carried[here]).astype(BF16)
-            vg_ref[here, lanes] = (mm_tn(mix_ref[h, tail, here], grad[tail]) + value_carried[here]).astype(BF16)
-        for n, (ref, hbm) in enumerate(((qg_ref, qg_hbm), (kg_ref, kg_hbm), (vg_ref, vg_hbm))):
-            lanes = pl.ds(h * HD, HD)
-            copies.append(pltpu.make_async_copy(ref.at[:, lanes], hbm.at[:, lanes], sems.at[n, h]))
-            copies[-1].start()
+    rests = jnp.exp(col_ref[length - 1 : length] - col_ref[...])
+    for pair in range(kg_ref.shape[1] // (2 * HD)):
+        back = diagonal(back_ref, pair)
+        key_pair = mm_nt(two_heads(v_ref, pair), back)
+        value_pair = mm(two_heads(k_ref, pair), back)
+        for n in range(2):
+            h = 2 * pair + n
+            lanes, mine, rest = slice(h * HD, (h + 1) * HD), slice(n * HD, (n + 1) * HD), rests[:, h : h + 1]
+            kg_ref[:, lanes] = (kacc_ref[:, lanes].astype(F32) + rest * key_pair[:, mine]).astype(BF16)
+            vg_ref[:, lanes] = (vacc_ref[:, lanes].astype(F32) + rest * value_pair[:, mine]).astype(BF16)
+            for m, (ref, hbm) in enumerate(((kg_ref, kg_hbm), (vg_ref, vg_hbm))):
+                lanes = pl.ds(h * HD, HD)
+                copies.append(pltpu.make_async_copy(ref.at[:, lanes], hbm.at[:, lanes], sems.at[m, h]))
+                copies[-1].start()
     for copy in copies:
         copy.wait()
 
@@ -309,7 +349,7 @@
 VMEM, SMEM, HBM = (pl.BlockSpec(memory_space=space) for space in (pltpu.VMEM, pltpu.SMEM, pltpu.HBM))
 
 
-def call(kernel, outs, *args, ins=None, out_specs=None, scratch=(), vmem=16 * 1024 * 1024):
+def call(kernel, outs, *args, ins=None, out_specs=None, scratch=(), vmem=16 * 1024 * 1024, flops=0, moved=0):
     return pl.pallas_call(
         kernel,
         out_shape=[jax.ShapeDtypeStruct(shape, dtype) for shape, dtype in outs],
@@ -317,6 +357,7 @@
         out_specs=out_specs or [VMEM] * len(outs),
         scratch_shapes=list(scratch),
         compiler_params=pltpu.CompilerParams(vmem_limit_bytes=vmem),
+        cost_estimate=pl.CostEstimate(flops=flops, bytes_accessed=moved, transcendentals=0) if flops else None,
     )(*args)
 
 
@@ -353,13 +394,18 @@
         spread_kernel, [piece, scalars], group, near, far, totals, ins=[SMEM] + [VMEM] * 3
     )
     state = exchange(send, NEAR).reshape(features, HD)
-    cum_rows, mixes = ((heads, length), F32), ((heads, length, length), BF16)
-    attention, sums, mix, row, col = call(
+    inner, row, col, gain_row = call(
+        inner_kernel,
+        [whole, ((heads, length), F32), columns, ((1, features), F32)],
+        *in_hbm(queries, keys, values, gain_row), decay_rows, *in_hbm(send),
+        ins=[HBM] * 4 + [VMEM, HBM],
+        scratch=[staging] * 3 + [dma((3, heads // 2)), dma],
+        flops=2_000_000_000, moved=3_000_000,
+    )
+    attention, sums = call(
         attention_kernel,
-        [whole, ((8, SIDE, HD), F32), mixes, cum_rows, columns],
-        queries, keys, values, out_grad, gain_row, decay_rows, state,
-        ins=[VMEM] * 4 + [HBM] + [VMEM] * 2,
-        scratch=[pltpu.VMEM((1, features), F32), dma],
+        [whole, ((8, SIDE, HD), F32)],
+        queries, out_grad, gain_row, inner, col, state,
     )
     sums = lax.all_to_all(sums, "tp", 0, 0, tiled=True)
     grad, send = call(
@@ -370,21 +416,33 @@
     near = exchange(send, NEAR)
     (send,) = call(back_group_kernel, [message], near, totals)
     far = exchange(send, FAR)
+    query_grad, key_part, value_part = call(
+        local_grad_kernel,
+        [half, half, half],
+        *in_hbm(queries, keys, values), grad, row, col, state, *in_hbm(send),
+        ins=[HBM] * 3 + [VMEM] * 4 + [HBM],
+        out_specs=[HBM, VMEM, VMEM],
+        scratch=[staging] * 4
+        + [pltpu.VMEM((length, length), BF16)] * 2
+        + [dma((3, heads // 2)), dma((heads,))],
+        flops=4_000_000_000, moved=5_000_000,
+    )
     send, gain_grad = call(
         back_spread_kernel,
         [piece, ((1, HD), F32)],
-        group, near, far, totals, far_totals,
-        ins=[SMEM] + [VMEM] * 4,
+        group, near, far, totals, far_totals, *in_hbm(query_grad),
+        ins=[SMEM] + [VMEM] * 4 + [HBM],
     )
     back = exchange(send, NEAR).reshape(features, HD)
     gain_out = ((features // (SIDE * SIDE),), F32)
-    return call(
+    key_grad, value_grad, gain_grad = call(
         final_kernel,
-        [half, half, half, gain_out],
-        queries, keys, values, grad, mix, row, col, state, back, gain_grad,
-        out_specs=[HBM] * 4,
-        scratch=[staging] * 3 + [pltpu.VMEM(*gain_out), pltpu.VMEM((length, length), BF16), dma((3, heads)), dma],
-    )
+        [half, half, gain_out],
+        keys, values, col, back, key_part, value_part, gain_grad,
+        out_specs=[HBM] * 3,
+        scratch=[staging] * 2 + [pltpu.VMEM(*gain_out), dma((2, heads)), dma],
+    )
+    return query_grad, key_grad, value_grad, gain_grad
 
 
 def solution(mesh):

time: 116 us -> 115 us (level)
  blocking collectives: 105 us -> 75.2 us
  waiting for transfers between devices: 0 us -> 12.8 us
  starting transfers between devices: 0 us -> 11 us
  Pallas kernels: 9.66 us -> 14.7 us
    all_to_all x6 -> x4, blocking collectives: 96.3 us -> 66.2 us  [exchange(): lax.all_to_all(parts, 'seq', 0, 0, tiled=True, axis_index_groups=groups)]
    all_to_all x0 -> x2, waiting for transfers between devices: none -> 12.8 us  [exchange(): lax.all_to_all(parts, 'seq', 0, 0, tiled=True, axis_index_groups=groups)]
    all_to_all x0 -> x2, starting transfers between devices: none -> 11 us  [exchange(): lax.all_to_all(parts, 'seq', 0, 0, tiled=True, axis_index_groups=groups)]
    pallas_call x8 -> x10, Pallas kernels: 9.66 us -> 14.7 us  [call(): pl.pallas_call(kernel, out_shape=[jax.ShapeDtypeStruct(shape, dtype) for...]
  transfers between devices with their start and end apart: 0 -> 2, of which waited for: 0 -> 2; matrix products, arithmetic and copies ran while one was open for 0% -> 0% of each run, Pallas kernels for 0% -> 6%
where the time goes in v4:
time: 115 us; the launch traced here: 114 us
  blocking collectives  75.2 us (65%)
  Pallas kernels  14.7 us (13%)
  waiting for transfers between devices  12.8 us (11%)
  starting transfers between devices  11 us (10%)
    all_to_all x4, blocking collectives, exchange(): lax.all_to_all(parts, 'seq', 0, 0, tiled=True, axis_index_groups=groups)  66.2 us
    pallas_call x10, Pallas kernels, call(): pl.pallas_call(kernel, out_shape=[jax.ShapeDtypeStruct(shape, dtype) for...  14.7 us
    all_to_all x2, waiting for transfers between devices, exchange(): lax.all_to_all(parts, 'seq', 0, 0, tiled=True, axis_index_groups=groups)  12.8 us
    all_to_all x2, starting transfers between devices, exchange(): lax.all_to_all(parts, 'seq', 0, 0, tiled=True, axis_index_groups=groups)  11 us
    all_to_all x1, blocking collectives, shards(): sums = lax.all_to_all(sums, 'tp', 0, 0, tiled=True)  9.03 us
  transfers between devices with their start and end apart: 2, of which 2 were waited for; matrix products, arithmetic and copies ran while one was open for 0% of the time, Pallas kernels for 6%

profile of v4, /device:TPU:1, one launch (start us, length us, event | category | flops | bytes accessed | tf_op | source)
XLA Modules:
  0.0 114.4 jit_solution(9573463734009340653)
XLA Ops:
  0.6 2.2 %shard_map.93 = bf16[8,72,128]{2,1,0:T(8,128)(2,1)S(1)} custom-call(s32[1]{0:T(128)} %bitcast.2.me_ref, bf16[512,512]{1,0:T(8,128)(2,1)} %k_ref.1, bf16[512,512]{1,0:T(8,128)(2,1)} %v_ref.1, f32[4,512]{1,0:T(4,128)} %bitcast.8), custom_call_target="tpu_custom_call" | custom-call | tf_op jit(solution)/shard_map/pallas_call | solution.py:353
  2.9 15.2 %all_to_all.35.got_ref = bf16[8,72,128]{2,1,0:T(8,128)(2,1)S(1)} all-to-all(bf16[8,72,128]{2,1,0:T(8,128)(2,1)S(1)} %shard_map.93), channel_id=1, replica_groups={{0,8,16,24,32,40,48,56},{64,72,80,88,96,104,112,120},{128,136,144,152,1..., dimensions={0} | all-to-all | bytes 294912 | tf_op jit(solution)/shard_map/all_to_all | solution.py:369
  18.1 27.0 %all_to_all.36.far_ref = bf16[8,72,128]{2,1,0:T(8,128)(2,1)S(1)} all-to-all(bf16[8,72,128]{2,1,0:T(8,128)(2,1)S(1)} %get-tuple-element.24), channel_id=1, replica_groups={{0,64,128,192,256,320,384,448},{8,72,136,200,264,328,392,456},{16,80,14..., dimensions={0} | all-to-all | bytes 294912 | tf_op jit(solution)/shard_map/all_to_all | solution.py:369
  45.1 0.7 shard_map.95
  45.9 0.0 copy-start.4
  45.9 7.6 %all-to-all-start.2 = ((bf16[8,64,128]{2,1,0:T(8,128)(2,1)}), bf16[8,64,128]{2,1,0:T(8,128)(2,1)S(1)}, u32[]{:S(2)}, u32[]{:S(2)}) async-start(bf16[8,64,128]{2,1,0:T(8,128)(2,1)} %get-tuple-element.26.after_ref), calls=%async_computation.2 | async-start | bytes 262144 | tf_op jit(solution)/shard_map/all_to_all | solution.py:369
  53.5 0.0 copy-done.4
  53.5 2.9 %shard_map.96 = (f32[512,512]{1,0:T(8,128)S(1)}, f32[4,512]{1,0:T(4,128)S(1)}, f32[512,8]{1,0:T(8,128)S(1)}, f32[1,512]{1,0:T(1,128)S(1)}) custom-call(bf16[512,512]{1,0:T(8,128)(2,1)} %q_hbm.3, bf16[512,512]{1,0:T(8,128)(2,1)} %k_ref.1, bf16[512,512]{1,0:T(8,128)(2,1)} %v_ref.1, f32[1,512]{1,0:T(1,128)} %bitcast.10, f32[4,512]{1,0:T(4,128)S(1)} %bitcast.9, ...), custom_call_target="tpu_custom_call" | custom-call | flops 2000000000 | bytes 3000000 | tf_op jit(solution)/shard_map/pallas_call | solution.py:353
  56.3 2.9 %all-to-all-done.2 = bf16[8,64,128]{2,1,0:T(8,128)(2,1)S(1)} async-done(((bf16[8,64,128]{2,1,0:T(8,128)(2,1)}), bf16[8,64,128]{2,1,0:T(8,128)(2,1)S(1)}, u32[]{:S(2)}, u32[]{:S(2)}) %all-to-all-start.2) | async-done | bytes 131104 | tf_op jit(solution)/shard_map/all_to_all | solution.py:369
  59.3 0.0 copy-done.2
  59.3 0.0 copy-done.3
  59.3 0.7 shard_map.97
  59.9 9.0 %all_to_all.37.sums_ref = f32[8,8,128]{2,1,0:T(8,128)S(1)} all-to-all(f32[8,8,128]{2,1,0:T(8,128)S(1)} %get-tuple-element.30), channel_id=1, replica_groups=mesh['seq'=64,'tp'=8] {'tp'}, dimensions={0} | all-to-all | bytes 65536 | tf_op jit(solution)/shard_map/all_to_all | solution.py:410
  69.0 1.2 %shard_map.98 = (bf16[512,512]{1,0:T(8,128)(2,1)S(1)}, bf16[8,72,128]{2,1,0:T(8,128)(2,1)S(1)}) custom-call(f32[8,8,128]{2,1,0:T(8,128)S(1)} %all_to_all.37.sums_ref, f32[512,512]{1,0:T(8,128)S(1)} %get-tuple-element.31.att_ref, bf16[512,512]{1,0:T(8,128)(2,1)S(1)} %copy-done.2, f32[1,512]{1,0:T(1,128)S(1)} %get-tuple-element.27.gain_ref, ...), custom_call_target="tpu_custom_call" | custom-call | tf_op jit(solution)/shard_map/pallas_call | solution.py:353
  70.2 10.8 %all_to_all.38.got_ref = bf16[8,72,128]{2,1,0:T(8,128)(2,1)S(1)} all-to-all(bf16[8,72,128]{2,1,0:T(8,128)(2,1)S(1)} %get-tuple-element.34), channel_id=1, replica_groups={{0,8,16,24,32,40,48,56},{64,72,80,88,96,104,112,120},{128,136,144,152,1..., dimensions={0} | all-to-all | bytes 294912 | tf_op jit(solution)/shard_map/all_to_all | solution.py:369
  81.0 0.8 shard_map.99.after_ref
  81.8 3.4 %all-to-all-start.5 = ((bf16[8,72,128]{2,1,0:T(8,128)(2,1)}), bf16[8,72,128]{2,1,0:T(8,128)(2,1)S(1)}, u32[]{:S(2)}, u32[]{:S(2)}) async-start(bf16[8,72,128]{2,1,0:T(8,128)(2,1)} %shard_map.99.after_ref), calls=%async_computation.5 | async-start | bytes 294912 | tf_op jit(solution)/shard_map/all_to_all | solution.py:369
  85.2 4.5 %shard_map.100 = (bf16[512,512]{1,0:T(8,128)(2,1)}, bf16[512,512]{1,0:T(8,128)(2,1)S(1)}, bf16[512,512]{1,0:T(8,128)(2,1)S(1)}) custom-call(bf16[512,512]{1,0:T(8,128)(2,1)} %q_hbm.3, bf16[512,512]{1,0:T(8,128)(2,1)} %k_ref.1, bf16[512,512]{1,0:T(8,128)(2,1)} %v_ref.1, bf16[512,512]{1,0:T(8,128)(2,1)S(1)} %get-tuple-element.32.grad_ref, ...), custom_call_target="tpu_custom_call" | custom-call | flops 4000000000 | bytes 5000000 | tf_op jit(solution)/shard_map/pallas_call | solution.py:353
  89.7 9.9 %all-to-all-done.5.far_ref = bf16[8,72,128]{2,1,0:T(8,128)(2,1)S(1)} async-done(((bf16[8,72,128]{2,1,0:T(8,128)(2,1)}), bf16[8,72,128]{2,1,0:T(8,128)(2,1)S(1)}, u32[]{:S(2)}, u32[]{:S(2)}) %all-to-all-start.5) | async-done | bytes 147488 | tf_op jit(solution)/shard_map/all_to_all | solution.py:369
  99.6 0.1 shard_map.101
  99.7 13.3 %all_to_all.39 = bf16[8,64,128]{2,1,0:T(8,128)(2,1)S(1)} all-to-all(bf16[8,64,128]{2,1,0:T(8,128)(2,1)S(1)} %get-tuple-element.37), channel_id=1, replica_groups={{0,8,16,24,32,40,48,56},{64,72,80,88,96,104,112,120},{128,136,144,152,1..., dimensions={0} | all-to-all | bytes 262144 | tf_op jit(solution)/shard_map/all_to_all | solution.py:369
  113.0 0.0 copy-done
  113.0 0.0 copy-done.1
  113.0 1.4 %shard_map.102 = (bf16[512,512]{1,0:T(8,128)(2,1)}, bf16[512,512]{1,0:T(8,128)(2,1)}, f32[8]{0:T(128)}) custom-call(bf16[512,512]{1,0:T(8,128)(2,1)S(1)} %copy-done, bf16[512,512]{1,0:T(8,128)(2,1)S(1)} %copy-done.1, f32[512,8]{1,0:T(8,128)S(1)} %get-tuple-element.29.col_ref, bf16[512,128]{1,0:T(8,128)(2,1)S(1)} %bitcast.7, ...), custom_call_target="tpu_custom_call" | custom-call | tf_op jit(solution)/shard_map/pallas_call | solution.py:353
  (5 shorter events, 0.1 us)
Async XLA Ops:
  45.9 7.6 %copy-start.4 = (f32[512,4]{0,1:T(4,128)S(1)}, f32[512,4]{0,1:T(4,128)}, u32[]{:S(2)}) copy-start(f32[512,4]{0,1:T(4,128)} %param.11) | copy-start | bytes 24580
  45.9 13.4 %all-to-all-start.2 = ((bf16[8,64,128]{2,1,0:T(8,128)(2,1)}), bf16[8,64,128]{2,1,0:T(8,128)(2,1)S(1)}, u32[]{:S(2)}, u32[]{:S(2)}) async-start(bf16[8,64,128]{2,1,0:T(8,128)(2,1)} %get-tuple-element.26.after_ref), calls=%async_computation.2 | async-start | bytes 262144 | tf_op jit(solution)/shard_map/all_to_all | solution.py:369
  53.5 5.8 %copy-start.2 = (bf16[512,512]{1,0:T(8,128)(2,1)S(1)}, bf16[512,512]{1,0:T(8,128)(2,1)}, u32[]{:S(2)}) copy-start(bf16[512,512]{1,0:T(8,128)(2,1)} %og_ref.3) | copy-start | bytes 1572868
  53.5 5.8 %copy-start.3 = (bf16[512,512]{1,0:T(8,128)(2,1)S(1)}, bf16[512,512]{1,0:T(8,128)(2,1)}, u32[]{:S(2)}) copy-start(bf16[512,512]{1,0:T(8,128)(2,1)} %q_hbm.3) | copy-start | bytes 1572868
  81.8 17.8 %all-to-all-start.5 = ((bf16[8,72,128]{2,1,0:T(8,128)(2,1)}), bf16[8,72,128]{2,1,0:T(8,128)(2,1)S(1)}, u32[]{:S(2)}, u32[]{:S(2)}) async-start(bf16[8,72,128]{2,1,0:T(8,128)(2,1)} %shard_map.99.after_ref), calls=%async_computation.5 | async-start | bytes 294912 | tf_op jit(solution)/shard_map/all_to_all | solution.py:369
  99.6 13.3 %copy-start = (bf16[512,512]{1,0:T(8,128)(2,1)S(1)}, bf16[512,512]{1,0:T(8,128)(2,1)}, u32[]{:S(2)}) copy-start(bf16[512,512]{1,0:T(8,128)(2,1)} %k_ref.1) | copy-start | bytes 1572868
  99.6 13.3 %copy-start.1 = (bf16[512,512]{1,0:T(8,128)(2,1)S(1)}, bf16[512,512]{1,0:T(8,128)(2,1)}, u32[]{:S(2)}) copy-start(bf16[512,512]{1,0:T(8,128)(2,1)} %v_ref.1) | copy-start | bytes 1572868

commit v5 on v4

--- a/solution.py
+++ b/solution.py
@@ -52,6 +52,11 @@
     for n, part in enumerate(parts):
         out = jnp.where(rows == n, part.astype(F32), out)
     return out.astype(BF16)
+
+
+def two_parts(rows):
+    high, mid, unused = split3(rows)
+    return jnp.concatenate([high.astype(F32), mid.astype(F32)], axis=0).astype(BF16)
 
 
 def read_scalar_row(tile):
@@ -126,7 +131,7 @@
 
 
 def spread_kernel(me_ref, got_ref, far_ref, tot_ref, send_ref, far_tot_ref):
-    group = me_ref[0]
+    group = lax.div(me_ref[0], SIDE)
     state = jnp.zeros((PIECE, HD), F32)
     for g in range(SIDE):
         total = read_scalar_row(far_ref[g, PIECE:])
@@ -139,28 +144,24 @@
 
 def back_group_kernel(got_ref, tot_ref, send_ref):
     acc = jnp.zeros((PIECE, HD), F32)
-    gain = jnp.zeros((1, HD), F32)
+    gain = jnp.zeros((MESSAGE - PIECE, HD), F32)
     for m in reversed(range(SIDE)):
         acc = jnp.exp(tot_ref[m : m + 1]) * acc + got_ref[m, :PIECE].astype(F32)
-        gain = gain + got_ref[m, PIECE:].astype(F32)[0:1]
-    feature = iota((HD, HD), 0)
-    lane = iota((HD, HD), 1)
-    pick = ((feature % 8) == lane).astype(BF16)
-    mine = ((iota((SIDE, HD), 1) % 64) // 8) == iota((SIDE, HD), 0)
-    picked = sum(mm(jnp.where(mine, part.astype(F32), 0.0).astype(BF16), pick) for part in split3(gain))
-    parts = split3(picked)
+        gain = gain + got_ref[m, PIECE:].astype(F32)
+    half = gain.shape[0] // 2
+    tile = two_parts(gain[:half] + gain[half:])
     acc = acc.astype(BF16)
     for g in range(SIDE):
         send_ref[g, :PIECE] = acc
-        send_ref[g, PIECE:] = rows_of(*(part[g : g + 1] for part in parts))
-
-
-def back_spread_kernel(me_ref, got_ref, far_ref, tot_ref, far_tot_ref, after_ref, send_ref, gain_ref):
-    group = me_ref[0]
+        send_ref[g, PIECE:] = tile
+
+
+def back_spread_kernel(me_ref, got_ref, far_ref, tot_ref, far_tot_ref, send_ref, gain_ref):
+    group = lax.div(me_ref[0], SIDE)
     state = jnp.zeros((PIECE, HD), F32)
-    gain = jnp.zeros((1, HD), F32)
+    gain = jnp.zeros((MESSAGE - PIECE, HD), F32)
     for g in reversed(range(SIDE)):
-        gain = gain + read_scalar_row(far_ref[g, PIECE:])
+        gain = gain + far_ref[g, PIECE:].astype(F32)
         state = jnp.where(g > group, jnp.exp(far_tot_ref[g : g + 1]) * state + far_ref[g, :PIECE].astype(F32), state)
     gain_ref[...] = gain
     for m in reversed(range(SIDE)):
@@ -187,7 +188,7 @@
 
 def inner_kernel(
     q_hbm, k_hbm, v_hbm, gain_hbm, ld_ref, after_ref,
-    inner_ref, row_ref, col_ref, gain_ref,
+    inner_ref, sq_ref, row_ref, col_ref, gain_ref,
     q_ref, k_ref, v_ref, sems, gain_sem,
 ):
     heads, length = ld_ref.shape
@@ -200,6 +201,7 @@
             copies.append(pltpu.make_async_copy(hbm.at[:, lanes], ref.at[:, lanes], sems.at[n, pair]))
             copies[-1].start()
     row_ref[...], col_ref[...] = cumulative(ld_ref)
+    grow = jnp.exp(col_ref[...])
     causal = causal_tile()
     for h in range(heads):
         if h % 2 == 0:
@@ -207,6 +209,7 @@
                 copy.wait()
         q, k, v = head(q_ref, h), head(k_ref, h), head(v_ref, h)
         col, row = col_ref[:, h : h + 1], row_ref[h : h + 1]
+        sq_ref[:, h * HD : (h + 1) * HD] = (q.astype(F32) * grow[:, h : h + 1]).astype(BF16)
         for i in range(length // BLOCK):
             here, wide = slice(i * BLOCK, (i + 1) * BLOCK), (i + 1) * BLOCK
             (mix,) = decayed([mm_nt(q[here], k[:wide])], col, row, i, causal)
@@ -214,17 +217,16 @@
     gain_copy.wait()
 
 
-def attention_kernel(q_ref, og_ref, gain_ref, inner_ref, col_ref, state_ref, att_ref, sums_ref):
-    length, features = q_ref.shape
+def attention_kernel(sq_ref, og_ref, gain_ref, inner_ref, state_ref, att_ref, sums_ref):
+    length, features = sq_ref.shape
     heads = features // HD
     count = length // TILE
-    grow = jnp.exp(col_ref[...])
     squares, dots = jnp.zeros((length, HD), F32), jnp.zeros((length, HD), F32)
     for h in range(heads):
         lanes, mine = slice(h * HD, (h + 1) * HD), slice(h % 2 * HD, (h % 2 + 1) * HD)
         if h % 2 == 0:
-            carried = mm(two_heads(q_ref, h // 2), diagonal(state_ref, h // 2))
-        att = inner_ref[:, lanes].astype(F32) + grow[:, h : h + 1] * carried[:, mine]
+            carried = mm(two_heads(sq_ref, h // 2), diagonal(state_ref, h // 2))
+        att = inner_ref[:, lanes] + carried[:, mine]
         att_ref[:, lanes] = att
         squares = squares + att * att
         dots = dots + att * (gain_ref[:, lanes] * og_ref[:, lanes].astype(F32))
@@ -239,7 +241,7 @@
         sums_ref[t] = sums
 
 
-def gradient_kernel(sums_ref, att_ref, og_ref, gain_ref, q_ref, col_ref, grad_ref, send_ref):
+def gradient_kernel(sums_ref, att_ref, og_ref, gain_ref, sq_ref, grad_ref, send_ref):
     length, features = att_ref.shape
     count = length // TILE
     sums = sums_ref[0]
@@ -256,48 +258,35 @@
     gains = []
     for h in range(features // HD):
         att = head(att_ref, h)
-        out_grad = head(og_ref, h).astype(F32)
-        upstream = gain_ref[:, h * HD : (h + 1) * HD] * out_grad
-        grad = (inverse * upstream - slope * att).astype(BF16)
+        normed = inverse * head(og_ref, h).astype(F32)
+        grad = (normed * gain_ref[:, h * HD : (h + 1) * HD] - slope * att).astype(BF16)
         grad_ref[:, h * HD : (h + 1) * HD] = grad
-        gains.append(jnp.sum(out_grad * att * inverse, axis=0, keepdims=True))
-        scaled = (head(q_ref, h).astype(F32) * jnp.exp(col_ref[:, h : h + 1])).astype(BF16)
-        update = mm_tn(scaled, grad).astype(BF16)
+        gains.append(jnp.sum(normed * att, axis=0, keepdims=True))
+        update = mm_tn(head(sq_ref, h), grad).astype(BF16)
         for half in range(2):
             send_ref[2 * h + half, :PIECE] = update[half * PIECE : (half + 1) * PIECE]
-    gain_part = jnp.concatenate(gains, axis=1)
-    high, mid, low = (part.astype(F32) for part in split3(gain_part))
-    mine = ((iota((SIDE, features), 1) // 8) % 8) == iota((SIDE, features), 0)
-    feature, lane = iota((features, HD), 0), iota((features, HD), 1)
-    place = (feature // 64) * 8 + feature % 8
-    to_high = (place == lane).astype(BF16)
-    to_low = (place + 64 == lane).astype(BF16)
-    picked = mm(jnp.where(mine, high, 0.0).astype(BF16), to_high) + mm(
-        jnp.where(mine, mid, 0.0).astype(BF16), to_low
-    )
+    tile = two_parts(jnp.concatenate(gains, axis=0))
     for m in range(SIDE):
-        send_ref[m, PIECE:] = rows_of(picked[m : m + 1])
+        send_ref[m, PIECE:] = tile
 
 
 def local_grad_kernel(
-    q_hbm, k_hbm, v_hbm, grad_ref, row_ref, col_ref, state_ref, after_ref,
+    q_hbm, k_ref, v_ref, grad_ref, row_ref, col_ref, state_ref, after_ref,
     qg_hbm, kacc_ref, vacc_ref,
-    q_ref, k_ref, v_ref, qg_ref, mix_ref, gmix_ref, sems, out_sems,
+    q_ref, qg_ref, mix_ref, gmix_ref, sems, out_sems,
 ):
     heads, length = row_ref.shape
     ins, outs = [], []
     for pair in range(heads // 2):
         lanes = pl.ds(2 * pair * HD, 2 * HD)
-        for n, (hbm, ref) in enumerate(((v_hbm, v_ref), (k_hbm, k_ref), (q_hbm, q_ref))):
-            ins.append(pltpu.make_async_copy(hbm.at[:, lanes], ref.at[:, lanes], sems.at[n, pair]))
-            ins[-1].start()
+        ins.append(pltpu.make_async_copy(q_hbm.at[:, lanes], q_ref.at[:, lanes], sems.at[pair]))
+        ins[-1].start()
     causal = causal_tile()
     grow = jnp.exp(col_ref[...])
     for h in range(heads):
         if h % 2 == 0:
             query_pair = mm_nt(two_heads(grad_ref, h // 2), diagonal(state_ref, h // 2))
-            for copy in ins[3 * (h // 2) : 3 * (h // 2 + 1)]:
-                copy.wait()
+            ins[h // 2].wait()
         lanes, mine = slice(h * HD, (h + 1) * HD), slice(h % 2 * HD, (h % 2 + 1) * HD)
         q, k, v, grad = head(q_ref, h), head(k_ref, h), head(v_ref, h), head(grad_ref, h)
         col, row = col_ref[:, h : h + 1], row_ref[h : h + 1]
@@ -320,12 +309,20 @@
 
 
 def final_kernel(
-    k_ref, v_ref, col_ref, back_ref, kacc_ref, vacc_ref, gain_row_ref,
+    me_ref, k_ref, v_ref, col_ref, back_ref, kacc_ref, vacc_ref, gain_rows_ref,
     kg_hbm, vg_hbm, gain_hbm,
     kg_ref, vg_ref, gain_ref, sems, gain_sem,
 ):
     length = col_ref.shape[0]
-    gain_ref[...] = gain_row_ref[0, : gain_ref.shape[0]]
+    count = gain_ref.shape[0]
+    parts, rows = gain_rows_ref[...], gain_rows_ref.shape[0] // 2
+    gains = parts[:rows] + parts[rows:]
+    start = me_ref[0] * count
+    row = jnp.zeros((1, HD), F32)
+    for n in range(rows):
+        row = jnp.where(n == start // HD, gains[n : n + 1], row)
+    row = pltpu.roll(jnp.broadcast_to(row, (8, HD)), lax.rem(HD - lax.rem(start, HD), HD), 1)
+    gain_ref[...] = row[0, :count]
     copies = [pltpu.make_async_copy(gain_ref, gain_hbm, gain_sem)]
     copies[0].start()
     rests = jnp.exp(col_ref[length - 1 : length] - col_ref[...])
@@ -374,7 +371,7 @@
     heads = features // HD
     gain_row = gain.reshape(1, features)
     decay_rows = log_decay.T
-    group = (lax.axis_index("seq") // SIDE).astype(jnp.int32).reshape(1)
+    place = lax.axis_index("seq").astype(jnp.int32).reshape(1)
     message = ((SIDE, MESSAGE, HD), BF16)
     piece = ((SIDE, PIECE, HD), BF16)
     scalars = ((SIDE, HD), F32)
@@ -383,7 +380,7 @@
     (send,) = call(
         update_kernel,
         [message],
-        group, *in_hbm(keys, values, decay_rows),
+        place, *in_hbm(keys, values, decay_rows),
         ins=[SMEM, HBM, HBM, HBM],
         scratch=[staging, staging, pltpu.VMEM((heads, length), F32), dma((2, length // TILE)), dma],
     )
@@ -391,12 +388,12 @@
     send, totals = call(group_kernel, [message, scalars], near)
     far = exchange(send, FAR)
     send, far_totals = call(
-        spread_kernel, [piece, scalars], group, near, far, totals, ins=[SMEM] + [VMEM] * 3
+        spread_kernel, [piece, scalars], place, near, far, totals, ins=[SMEM] + [VMEM] * 3
     )
     state = exchange(send, NEAR).reshape(features, HD)
-    inner, row, col, gain_row = call(
+    inner, scaled, row, col, gain_row = call(
         inner_kernel,
-        [whole, ((heads, length), F32), columns, ((1, features), F32)],
+        [whole, half, ((heads, length), F32), columns, ((1, features), F32)],
         *in_hbm(queries, keys, values, gain_row), decay_rows, *in_hbm(send),
         ins=[HBM] * 4 + [VMEM, HBM],
         scratch=[staging] * 3 + [dma((3, heads // 2)), dma],
@@ -405,40 +402,41 @@
     attention, sums = call(
         attention_kernel,
         [whole, ((8, SIDE, HD), F32)],
-        queries, out_grad, gain_row, inner, col, state,
+        scaled, out_grad, gain_row, inner, state,
     )
     sums = lax.all_to_all(sums, "tp", 0, 0, tiled=True)
     grad, send = call(
         gradient_kernel,
         [half, message],
-        sums, attention, out_grad, gain_row, queries, col,
+        sums, attention, out_grad, gain_row, scaled,
     )
     near = exchange(send, NEAR)
     (send,) = call(back_group_kernel, [message], near, totals)
     far = exchange(send, FAR)
+    send, gain_grad = call(
+        back_spread_kernel,
+        [piece, scalars],
+        place, near, far, totals, far_totals,
+        ins=[SMEM] + [VMEM] * 4,
+    )
     query_grad, key_part, value_part = call(
         local_grad_kernel,
         [half, half, half],
-        *in_hbm(queries, keys, values), grad, row, col, state, *in_hbm(send),
-        ins=[HBM] * 3 + [VMEM] * 4 + [HBM],
+        *in_hbm(queries), keys, values, grad, row, col, state, *in_hbm(send),
+        ins=[HBM] + [VMEM] * 6 + [HBM],
         out_specs=[HBM, VMEM, VMEM],
-        scratch=[staging] * 4
+        scratch=[staging] * 2
         + [pltpu.VMEM((length, length), BF16)] * 2
-        + [dma((3, heads // 2)), dma((heads,))],
+        + [dma((heads // 2,)), dma((heads,))],
         flops=4_000_000_000, moved=5_000_000,
-    )
-    send, gain_grad = call(
-        back_spread_kernel,
-        [piece, ((1, HD), F32)],
-        group, near, far, totals, far_totals, *in_hbm(query_grad),
-        ins=[SMEM] + [VMEM] * 4 + [HBM],
     )
     back = exchange(send, NEAR).reshape(features, HD)
     gain_out = ((features // (SIDE * SIDE),), F32)
     key_grad, value_grad, gain_grad = call(
         final_kernel,
         [half, half, gain_out],
-        keys, values, col, back, key_part, value_part, gain_grad,
+        place, keys, values, col, back, key_part, value_part, gain_grad,
+        ins=[SMEM] + [VMEM] * 7,
         out_specs=[HBM] * 3,
         scratch=[staging] * 2 + [pltpu.VMEM(*gain_out), dma((2, heads)), dma],
     )

time: 115 us -> 114 us (level)
  waiting for transfers between devices: 12.8 us -> 4.44 us
  starting transfers between devices: 11 us -> 15.1 us
  blocking collectives: 75.2 us -> 79.3 us
    all_to_all x2, waiting for transfers between devices: 12.8 us -> 4.44 us  [exchange(): lax.all_to_all(parts, 'seq', 0, 0, tiled=True, axis_index_groups=groups)]
    all_to_all x4, blocking collectives: 66.2 us -> 70.3 us  [exchange(): lax.all_to_all(parts, 'seq', 0, 0, tiled=True, axis_index_groups=groups)]
    all_to_all x2, starting transfers between devices: 11 us -> 15.1 us  [exchange(): lax.all_to_all(parts, 'seq', 0, 0, tiled=True, axis_index_groups=groups)]
where the time goes in v5:
time: 114 us; the launch traced here: 113 us
  blocking collectives  79.3 us (70%)
  starting transfers between devices  15.1 us (13%)
  Pallas kernels  13.6 us (12%)
  waiting for transfers between devices  4.44 us (4%)
    all_to_all x4, blocking collectives, exchange(): lax.all_to_all(parts, 'seq', 0, 0, tiled=True, axis_index_groups=groups)  70.3 us
    all_to_all x2, starting transfers between devices, exchange(): lax.all_to_all(parts, 'seq', 0, 0, tiled=True, axis_index_groups=groups)  15.1 us
    pallas_call x10, Pallas kernels, call(): pl.pallas_call(kernel, out_shape=[jax.ShapeDtypeStruct(shape, dtype) for...  13.6 us
    all_to_all x1, blocking collectives, shards(): sums = lax.all_to_all(sums, 'tp', 0, 0, tiled=True)  9.02 us
    all_to_all x2, waiting for transfers between devices, exchange(): lax.all_to_all(parts, 'seq', 0, 0, tiled=True, axis_index_groups=groups)  4.44 us
  transfers between devices with their start and end apart: 2, of which 2 were waited for; matrix products, arithmetic and copies ran while one was open for 0% of the time, Pallas kernels for 6%

profile of v5, /device:TPU:1, one launch (start us, length us, event | category | flops | bytes accessed | tf_op | source)
XLA Modules:
  0.0 113.2 jit_solution(668137806270612845)
XLA Ops:
  0.6 2.2 %shard_map.93 = bf16[8,72,128]{2,1,0:T(8,128)(2,1)S(1)} custom-call(s32[1]{0:T(128)} %bitcast.2.me_ref, bf16[512,512]{1,0:T(8,128)(2,1)} %k_ref.3, bf16[512,512]{1,0:T(8,128)(2,1)} %v_ref.3, f32[4,512]{1,0:T(4,128)} %bitcast.8), custom_call_target="tpu_custom_call" | custom-call | tf_op jit(solution)/shard_map/pallas_call | solution.py:350
  2.9 15.2 %all_to_all.35.got_ref = bf16[8,72,128]{2,1,0:T(8,128)(2,1)S(1)} all-to-all(bf16[8,72,128]{2,1,0:T(8,128)(2,1)S(1)} %shard_map.93), channel_id=1, replica_groups={{0,8,16,24,32,40,48,56},{64,72,80,88,96,104,112,120},{128,136,144,152,1..., dimensions={0} | all-to-all | bytes 294912 | tf_op jit(solution)/shard_map/all_to_all | solution.py:366
  18.1 27.0 %all_to_all.36.far_ref = bf16[8,72,128]{2,1,0:T(8,128)(2,1)S(1)} all-to-all(bf16[8,72,128]{2,1,0:T(8,128)(2,1)S(1)} %get-tuple-element.25), channel_id=1, replica_groups={{0,64,128,192,256,320,384,448},{8,72,136,200,264,328,392,456},{16,80,14..., dimensions={0} | all-to-all | bytes 294912 | tf_op jit(solution)/shard_map/all_to_all | solution.py:366
  45.1 0.7 shard_map.95
  45.9 0.0 copy-start.3
  45.9 7.6 %all-to-all-start.2 = ((bf16[8,64,128]{2,1,0:T(8,128)(2,1)}), bf16[8,64,128]{2,1,0:T(8,128)(2,1)S(1)}, u32[]{:S(2)}, u32[]{:S(2)}) async-start(bf16[8,64,128]{2,1,0:T(8,128)(2,1)} %get-tuple-element.27.after_ref), calls=%async_computation.2 | async-start | bytes 262144 | tf_op jit(solution)/shard_map/all_to_all | solution.py:366
  53.5 0.0 copy-done.3
  53.5 0.0 copy-start
  53.5 2.8 %shard_map.96 = (f32[512,512]{1,0:T(8,128)S(1)}, bf16[512,512]{1,0:T(8,128)(2,1)S(1)}, f32[4,512]{1,0:T(4,128)S(1)}, f32[512,8]{1,0:T(8,128)S(1)}, f32[1,512]{1,0:T(1,128)S(1)}) custom-call(bf16[512,512]{1,0:T(8,128)(2,1)} %q_hbm.3, bf16[512,512]{1,0:T(8,128)(2,1)} %k_ref.3, bf16[512,512]{1,0:T(8,128)(2,1)} %v_ref.3, f32[1,512]{1,0:T(1,128)} %bitcast.10, ...), custom_call_target="tpu_custom_call" | custom-call | flops 2000000000 | bytes 3000000 | tf_op jit(solution)/shard_map/pallas_call | solution.py:350
  56.3 3.0 %all-to-all-done.2 = bf16[8,64,128]{2,1,0:T(8,128)(2,1)S(1)} async-done(((bf16[8,64,128]{2,1,0:T(8,128)(2,1)}), bf16[8,64,128]{2,1,0:T(8,128)(2,1)S(1)}, u32[]{:S(2)}, u32[]{:S(2)}) %all-to-all-start.2) | async-done | bytes 131104 | tf_op jit(solution)/shard_map/all_to_all | solution.py:366
  59.3 0.0 copy-done
  59.3 0.5 shard_map.97
  59.8 9.0 %all_to_all.37.sums_ref = f32[8,8,128]{2,1,0:T(8,128)S(1)} all-to-all(f32[8,8,128]{2,1,0:T(8,128)S(1)} %get-tuple-element.31), channel_id=1, replica_groups=mesh['seq'=64,'tp'=8] {'tp'}, dimensions={0} | all-to-all | bytes 65536 | tf_op jit(solution)/shard_map/all_to_all | solution.py:407
  68.8 0.8 shard_map.98
  69.6 10.8 %all_to_all.38.got_ref = bf16[8,72,128]{2,1,0:T(8,128)(2,1)S(1)} all-to-all(bf16[8,72,128]{2,1,0:T(8,128)(2,1)S(1)} %get-tuple-element.36), channel_id=1, replica_groups={{0,8,16,24,32,40,48,56},{64,72,80,88,96,104,112,120},{128,136,144,152,1..., dimensions={0} | all-to-all | bytes 294912 | tf_op jit(solution)/shard_map/all_to_all | solution.py:366
  80.4 0.0 copy-start.1
  80.4 17.4 %all_to_all.39.far_ref = bf16[8,72,128]{2,1,0:T(8,128)(2,1)S(1)} all-to-all(bf16[8,72,128]{2,1,0:T(8,128)(2,1)S(1)} %shard_map.99), channel_id=1, replica_groups={{0,64,128,192,256,320,384,448},{8,72,136,200,264,328,392,456},{16,80,14..., dimensions={0} | all-to-all | bytes 294912 | tf_op jit(solution)/shard_map/all_to_all | solution.py:366
  97.8 0.7 shard_map.100
  98.5 7.5 %all-to-all-start.6 = ((bf16[8,64,128]{2,1,0:T(8,128)(2,1)}), bf16[8,64,128]{2,1,0:T(8,128)(2,1)S(1)}, u32[]{:S(2)}, u32[]{:S(2)}) async-start(bf16[8,64,128]{2,1,0:T(8,128)(2,1)} %get-tuple-element.38.after_ref), calls=%async_computation.6 | async-start | bytes 262144 | tf_op jit(solution)/shard_map/all_to_all | solution.py:366
  106.0 0.0 copy-done.1
  106.0 0.0 copy-done.2
  106.0 4.3 %shard_map.101 = (bf16[512,512]{1,0:T(8,128)(2,1)}, bf16[512,512]{1,0:T(8,128)(2,1)S(1)}, bf16[512,512]{1,0:T(8,128)(2,1)S(1)}) custom-call(bf16[512,512]{1,0:T(8,128)(2,1)} %q_hbm.3, bf16[512,512]{1,0:T(8,128)(2,1)S(1)} %copy-done.1, bf16[512,512]{1,0:T(8,128)(2,1)S(1)} %copy-done.2, bf16[512,512]{1,0:T(8,128)(2,1)S(1)} %get-tuple-element.33.grad_ref, ...), custom_call_target="tpu_custom_call" | custom-call | flops 4000000000 | bytes 5000000 | tf_op jit(solution)/shard_map/pallas_call | solution.py:350
  110.3 1.5 %all-to-all-done.6 = bf16[8,64,128]{2,1,0:T(8,128)(2,1)S(1)} async-done(((bf16[8,64,128]{2,1,0:T(8,128)(2,1)}), bf16[8,64,128]{2,1,0:T(8,128)(2,1)S(1)}, u32[]{:S(2)}, u32[]{:S(2)}) %all-to-all-start.6) | async-done | bytes 131104 | tf_op jit(solution)/shard_map/all_to_all | solution.py:366
  111.8 1.4 %shard_map.102 = (bf16[512,512]{1,0:T(8,128)(2,1)}, bf16[512,512]{1,0:T(8,128)(2,1)}, f32[8]{0:T(128)}) custom-call(s32[1]{0:T(128)} %bitcast.2.me_ref, bf16[512,512]{1,0:T(8,128)(2,1)S(1)} %copy-done.1, bf16[512,512]{1,0:T(8,128)(2,1)S(1)} %copy-done.2, f32[512,8]{1,0:T(8,128)S(1)} %get-tuple-element.35.col_ref, bf16[512,128]{1,0:T(8,128)(2,1)S(1)} %bitcast.7, ...), custom_call_target="tpu_custom_call" | custom-call | tf_op jit(solution)/shard_map/pallas_call | solution.py:350
  (3 shorter events, 0.1 us)
Async XLA Ops:
  45.9 7.6 %copy-start.3 = (f32[512,4]{0,1:T(4,128)S(1)}, f32[512,4]{0,1:T(4,128)}, u32[]{:S(2)}) copy-start(f32[512,4]{0,1:T(4,128)} %param.11) | copy-start | bytes 24580
  45.9 13.4 %all-to-all-start.2 = ((bf16[8,64,128]{2,1,0:T(8,128)(2,1)}), bf16[8,64,128]{2,1,0:T(8,128)(2,1)S(1)}, u32[]{:S(2)}, u32[]{:S(2)}) async-start(bf16[8,64,128]{2,1,0:T(8,128)(2,1)} %get-tuple-element.27.after_ref), calls=%async_computation.2 | async-start | bytes 262144 | tf_op jit(solution)/shard_map/all_to_all | solution.py:366
  53.5 5.8 %copy-start = (bf16[512,512]{1,0:T(8,128)(2,1)S(1)}, bf16[512,512]{1,0:T(8,128)(2,1)}, u32[]{:S(2)}) copy-start(bf16[512,512]{1,0:T(8,128)(2,1)} %og_ref.3) | copy-start | bytes 1572868
  80.4 25.6 %copy-start.1 = (bf16[512,512]{1,0:T(8,128)(2,1)S(1)}, bf16[512,512]{1,0:T(8,128)(2,1)}, u32[]{:S(2)}) copy-start(bf16[512,512]{1,0:T(8,128)(2,1)} %k_ref.3) | copy-start | bytes 1572868
  80.4 25.6 %copy-start.2 = (bf16[512,512]{1,0:T(8,128)(2,1)S(1)}, bf16[512,512]{1,0:T(8,128)(2,1)}, u32[]{:S(2)}) copy-start(bf16[512,512]{1,0:T(8,128)(2,1)} %v_ref.3) | copy-start | bytes 1572868
  98.5 13.3 %all-to-all-start.6 = ((bf16[8,64,128]{2,1,0:T(8,128)(2,1)}), bf16[8,64,128]{2,1,0:T(8,128)(2,1)S(1)}, u32[]{:S(2)}, u32[]{:S(2)}) async-start(bf16[8,64,128]{2,1,0:T(8,128)(2,1)} %get-tuple-element.38.after_ref), calls=%async_computation.6 | async-start | bytes 262144 | tf_op jit(solution)/shard_map/all_to_all | solution.py:366

commit v6 on v5

--- a/solution.py
+++ b/solution.py
@@ -9,7 +9,7 @@
 HD = 128
 SIDE = 8
 PIECE = 64
-MESSAGE = PIECE + 8
+MESSAGE = PIECE + 16
 TILE = 128
 BLOCK = 256
 BF16, F32 = jnp.bfloat16, jnp.float32
@@ -56,7 +56,8 @@
 
 def two_parts(rows):
     high, mid, unused = split3(rows)
-    return jnp.concatenate([high.astype(F32), mid.astype(F32)], axis=0).astype(BF16)
+    rest = jnp.zeros((MESSAGE - PIECE - 2 * rows.shape[0], HD), F32)
+    return jnp.concatenate([high.astype(F32), mid.astype(F32), rest], axis=0).astype(BF16)
 
 
 def read_scalar_row(tile):
@@ -148,8 +149,7 @@
     for m in reversed(range(SIDE)):
         acc = jnp.exp(tot_ref[m : m + 1]) * acc + got_ref[m, :PIECE].astype(F32)
         gain = gain + got_ref[m, PIECE:].astype(F32)
-    half = gain.shape[0] // 2
-    tile = two_parts(gain[:half] + gain[half:])
+    tile = two_parts(gain[:4] + gain[4:8])
     acc = acc.astype(BF16)
     for g in range(SIDE):
         send_ref[g, :PIECE] = acc
@@ -163,7 +163,7 @@
     for g in reversed(range(SIDE)):
         gain = gain + far_ref[g, PIECE:].astype(F32)
         state = jnp.where(g > group, jnp.exp(far_tot_ref[g : g + 1]) * state + far_ref[g, :PIECE].astype(F32), state)
-    gain_ref[...] = gain
+    gain_ref[...] = gain[: gain_ref.shape[0]]
     for m in reversed(range(SIDE)):
         send_ref[m] = state.astype(BF16)
         state = jnp.exp(tot_ref[m : m + 1]) * state + got_ref[m, :PIECE].astype(F32)

time: 114 us -> 115 us (level)
  starting transfers between devices: 15.1 us -> 16.7 us
    all_to_all x2, starting transfers between devices: 15.1 us -> 16.7 us  [exchange(): lax.all_to_all(parts, 'seq', 0, 0, tiled=True, axis_index_groups=groups)]
where the time goes in v6:
time: 115 us
  blocking collectives  79.3 us (69%)
  starting transfers between devices  16.7 us (15%)
  Pallas kernels  13.7 us (12%)
  waiting for transfers between devices  4.44 us (4%)
    all_to_all x4, blocking collectives, exchange(): lax.all_to_all(parts, 'seq', 0, 0, tiled=True, axis_index_groups=groups)  70.3 us
    all_to_all x2, starting transfers between devices, exchange(): lax.all_to_all(parts, 'seq', 0, 0, tiled=True, axis_index_groups=groups)  16.7 us
    pallas_call x10, Pallas kernels, call(): pl.pallas_call(kernel, out_shape=[jax.ShapeDtypeStruct(shape, dtype) for...  13.7 us
    all_to_all x1, blocking collectives, shards(): sums = lax.all_to_all(sums, 'tp', 0, 0, tiled=True)  9.03 us
    all_to_all x2, waiting for transfers between devices, exchange(): lax.all_to_all(parts, 'seq', 0, 0, tiled=True, axis_index_groups=groups)  4.44 us
  transfers between devices with their start and end apart: 2, of which 2 were waited for; matrix products, arithmetic and copies ran while one was open for 0% of the time, Pallas kernels for 6%

profile of v6, /device:TPU:1, one launch (start us, length us, event | category | flops | bytes accessed | tf_op | source)
XLA Modules:
  0.0 114.9 jit_solution(80330978974939437)
XLA Ops:
  0.6 2.2 %shard_map.93 = bf16[8,80,128]{2,1,0:T(8,128)(2,1)S(1)} custom-call(s32[1]{0:T(128)} %bitcast.2.me_ref, bf16[512,512]{1,0:T(8,128)(2,1)} %k_ref.3, bf16[512,512]{1,0:T(8,128)(2,1)} %v_ref.3, f32[4,512]{1,0:T(4,128)} %bitcast.8), custom_call_target="tpu_custom_call" | custom-call | tf_op jit(solution)/shard_map/pallas_call | solution.py:350
  2.9 15.2 %all_to_all.35.got_ref = bf16[8,80,128]{2,1,0:T(8,128)(2,1)S(1)} all-to-all(bf16[8,80,128]{2,1,0:T(8,128)(2,1)S(1)} %shard_map.93), channel_id=1, replica_groups={{0,8,16,24,32,40,48,56},{64,72,80,88,96,104,112,120},{128,136,144,152,1..., dimensions={0} | all-to-all | bytes 327680 | tf_op jit(solution)/shard_map/all_to_all | solution.py:366
  18.2 27.0 %all_to_all.36.far_ref = bf16[8,80,128]{2,1,0:T(8,128)(2,1)S(1)} all-to-all(bf16[8,80,128]{2,1,0:T(8,128)(2,1)S(1)} %get-tuple-element.25), channel_id=1, replica_groups={{0,64,128,192,256,320,384,448},{8,72,136,200,264,328,392,456},{16,80,14..., dimensions={0} | all-to-all | bytes 327680 | tf_op jit(solution)/shard_map/all_to_all | solution.py:366
  45.1 0.7 shard_map.95
  45.9 0.0 copy-start.3
  45.9 8.4 %all-to-all-start.2 = ((bf16[8,64,128]{2,1,0:T(8,128)(2,1)}), bf16[8,64,128]{2,1,0:T(8,128)(2,1)S(1)}, u32[]{:S(2)}, u32[]{:S(2)}) async-start(bf16[8,64,128]{2,1,0:T(8,128)(2,1)} %get-tuple-element.27.after_ref), calls=%async_computation.2 | async-start | bytes 262144 | tf_op jit(solution)/shard_map/all_to_all | solution.py:366
  54.3 0.0 copy-done.3
  54.3 0.0 copy-start
  54.3 2.8 %shard_map.96 = (f32[512,512]{1,0:T(8,128)S(1)}, bf16[512,512]{1,0:T(8,128)(2,1)S(1)}, f32[4,512]{1,0:T(4,128)S(1)}, f32[512,8]{1,0:T(8,128)S(1)}, f32[1,512]{1,0:T(1,128)S(1)}) custom-call(bf16[512,512]{1,0:T(8,128)(2,1)} %q_hbm.3, bf16[512,512]{1,0:T(8,128)(2,1)} %k_ref.3, bf16[512,512]{1,0:T(8,128)(2,1)} %v_ref.3, f32[1,512]{1,0:T(1,128)} %bitcast.10, ...), custom_call_target="tpu_custom_call" | custom-call | flops 2000000000 | bytes 3000000 | tf_op jit(solution)/shard_map/pallas_call | solution.py:350
  57.1 3.0 %all-to-all-done.2 = bf16[8,64,128]{2,1,0:T(8,128)(2,1)S(1)} async-done(((bf16[8,64,128]{2,1,0:T(8,128)(2,1)}), bf16[8,64,128]{2,1,0:T(8,128)(2,1)S(1)}, u32[]{:S(2)}, u32[]{:S(2)}) %all-to-all-start.2) | async-done | bytes 131104 | tf_op jit(solution)/shard_map/all_to_all | solution.py:366
  60.1 0.0 copy-done
  60.1 0.5 shard_map.97
  60.6 9.0 %all_to_all.37.sums_ref = f32[8,8,128]{2,1,0:T(8,128)S(1)} all-to-all(f32[8,8,128]{2,1,0:T(8,128)S(1)} %get-tuple-element.31), channel_id=1, replica_groups=mesh['seq'=64,'tp'=8] {'tp'}, dimensions={0} | all-to-all | bytes 65536 | tf_op jit(solution)/shard_map/all_to_all | solution.py:407
  69.6 0.8 shard_map.98
  70.5 10.9 %all_to_all.38.got_ref = bf16[8,80,128]{2,1,0:T(8,128)(2,1)S(1)} all-to-all(bf16[8,80,128]{2,1,0:T(8,128)(2,1)S(1)} %get-tuple-element.36), channel_id=1, replica_groups={{0,8,16,24,32,40,48,56},{64,72,80,88,96,104,112,120},{128,136,144,152,1..., dimensions={0} | all-to-all | bytes 327680 | tf_op jit(solution)/shard_map/all_to_all | solution.py:366
  81.4 0.0 copy-start.1
  81.4 17.2 %all_to_all.39.far_ref = bf16[8,80,128]{2,1,0:T(8,128)(2,1)S(1)} all-to-all(bf16[8,80,128]{2,1,0:T(8,128)(2,1)S(1)} %shard_map.99), channel_id=1, replica_groups={{0,64,128,192,256,320,384,448},{8,72,136,200,264,328,392,456},{16,80,14..., dimensions={0} | all-to-all | bytes 327680 | tf_op jit(solution)/shard_map/all_to_all | solution.py:366
  98.6 0.7 shard_map.100
  99.3 8.3 %all-to-all-start.6 = ((bf16[8,64,128]{2,1,0:T(8,128)(2,1)}), bf16[8,64,128]{2,1,0:T(8,128)(2,1)S(1)}, u32[]{:S(2)}, u32[]{:S(2)}) async-start(bf16[8,64,128]{2,1,0:T(8,128)(2,1)} %get-tuple-element.38.after_ref), calls=%async_computation.6 | async-start | bytes 262144 | tf_op jit(solution)/shard_map/all_to_all | solution.py:366
  107.6 0.0 copy-done.2
  107.6 0.0 copy-done.1
  107.7 4.3 %shard_map.101 = (bf16[512,512]{1,0:T(8,128)(2,1)}, bf16[512,512]{1,0:T(8,128)(2,1)S(1)}, bf16[512,512]{1,0:T(8,128)(2,1)S(1)}) custom-call(bf16[512,512]{1,0:T(8,128)(2,1)} %q_hbm.3, bf16[512,512]{1,0:T(8,128)(2,1)S(1)} %copy-done.1, bf16[512,512]{1,0:T(8,128)(2,1)S(1)} %copy-done.2, bf16[512,512]{1,0:T(8,128)(2,1)S(1)} %get-tuple-element.33.grad_ref, ...), custom_call_target="tpu_custom_call" | custom-call | flops 4000000000 | bytes 5000000 | tf_op jit(solution)/shard_map/pallas_call | solution.py:350
  112.0 1.5 %all-to-all-done.6 = bf16[8,64,128]{2,1,0:T(8,128)(2,1)S(1)} async-done(((bf16[8,64,128]{2,1,0:T(8,128)(2,1)}), bf16[8,64,128]{2,1,0:T(8,128)(2,1)S(1)}, u32[]{:S(2)}, u32[]{:S(2)}) %all-to-all-start.6) | async-done | bytes 131104 | tf_op jit(solution)/shard_map/all_to_all | solution.py:366
  113.5 1.4 %shard_map.102 = (bf16[512,512]{1,0:T(8,128)(2,1)}, bf16[512,512]{1,0:T(8,128)(2,1)}, f32[8]{0:T(128)}) custom-call(s32[1]{0:T(128)} %bitcast.2.me_ref, bf16[512,512]{1,0:T(8,128)(2,1)S(1)} %copy-done.1, bf16[512,512]{1,0:T(8,128)(2,1)S(1)} %copy-done.2, f32[512,8]{1,0:T(8,128)S(1)} %get-tuple-element.35.col_ref, bf16[512,128]{1,0:T(8,128)(2,1)S(1)} %bitcast.7, ...), custom_call_target="tpu_custom_call" | custom-call | tf_op jit(solution)/shard_map/pallas_call | solution.py:350
  (3 shorter events, 0.1 us)
Async XLA Ops:
  45.9 8.4 %copy-start.3 = (f32[512,4]{0,1:T(4,128)S(1)}, f32[512,4]{0,1:T(4,128)}, u32[]{:S(2)}) copy-start(f32[512,4]{0,1:T(4,128)} %param.11) | copy-start | bytes 24580
  45.9 14.2 %all-to-all-start.2 = ((bf16[8,64,128]{2,1,0:T(8,128)(2,1)}), bf16[8,64,128]{2,1,0:T(8,128)(2,1)S(1)}, u32[]{:S(2)}, u32[]{:S(2)}) async-start(bf16[8,64,128]{2,1,0:T(8,128)(2,1)} %get-tuple-element.27.after_ref), calls=%async_computation.2 | async-start | bytes 262144 | tf_op jit(solution)/shard_map/all_to_all | solution.py:366
  54.3 5.8 %copy-start = (bf16[512,512]{1,0:T(8,128)(2,1)S(1)}, bf16[512,512]{1,0:T(8,128)(2,1)}, u32[]{:S(2)}) copy-start(bf16[512,512]{1,0:T(8,128)(2,1)} %og_ref.3) | copy-start | bytes 1572868
  81.3 26.3 %copy-start.2 = (bf16[512,512]{1,0:T(8,128)(2,1)S(1)}, bf16[512,512]{1,0:T(8,128)(2,1)}, u32[]{:S(2)}) copy-start(bf16[512,512]{1,0:T(8,128)(2,1)} %v_ref.3) | copy-start | bytes 1572868
  81.4 26.3 %copy-start.1 = (bf16[512,512]{1,0:T(8,128)(2,1)S(1)}, bf16[512,512]{1,0:T(8,128)(2,1)}, u32[]{:S(2)}) copy-start(bf16[512,512]{1,0:T(8,128)(2,1)} %k_ref.3) | copy-start | bytes 1572868
  99.3 14.1 %all-to-all-start.6 = ((bf16[8,64,128]{2,1,0:T(8,128)(2,1)}), bf16[8,64,128]{2,1,0:T(8,128)(2,1)S(1)}, u32[]{:S(2)}, u32[]{:S(2)}) async-start(bf16[8,64,128]{2,1,0:T(8,128)(2,1)} %get-tuple-element.38.after_ref), calls=%async_computation.6 | async-start | bytes 262144 | tf_op jit(solution)/shard_map/all_to_all | solution.py:366

commit v7 on v5

--- a/solution.py
+++ b/solution.py
@@ -12,6 +12,7 @@
 MESSAGE = PIECE + 8
 TILE = 128
 BLOCK = 256
+ROWS = 256
 BF16, F32 = jnp.bfloat16, jnp.float32
 
 NEAR = [[g * SIDE + m for m in range(SIDE)] for g in range(SIDE)]
@@ -107,8 +108,8 @@
     for copy in copies:
         copy.wait()
     for h in range(heads):
-        scaled = (head(k_ref, h).astype(F32) * rest[:, h : h + 1]).astype(BF16)
-        update = mm_tn(scaled, head(v_ref, h)).astype(BF16)
+        scaled = (head(v_ref, h).astype(F32) * rest[:, h : h + 1]).astype(BF16)
+        update = mm_tn(head(k_ref, h), scaled).astype(BF16)
         scalars = rows_of(*split3(jnp.broadcast_to(total[:, h : h + 1], (1, HD))))
         for half in range(2):
             send_ref[2 * h + half, :PIECE] = update[half * PIECE : (half + 1) * PIECE]
@@ -326,19 +327,21 @@
     copies = [pltpu.make_async_copy(gain_ref, gain_hbm, gain_sem)]
     copies[0].start()
     rests = jnp.exp(col_ref[length - 1 : length] - col_ref[...])
-    for pair in range(kg_ref.shape[1] // (2 * HD)):
-        back = diagonal(back_ref, pair)
-        key_pair = mm_nt(two_heads(v_ref, pair), back)
-        value_pair = mm(two_heads(k_ref, pair), back)
-        for n in range(2):
-            h = 2 * pair + n
-            lanes, mine, rest = slice(h * HD, (h + 1) * HD), slice(n * HD, (n + 1) * HD), rests[:, h : h + 1]
-            kg_ref[:, lanes] = (kacc_ref[:, lanes].astype(F32) + rest * key_pair[:, mine]).astype(BF16)
-            vg_ref[:, lanes] = (vacc_ref[:, lanes].astype(F32) + rest * value_pair[:, mine]).astype(BF16)
-            for m, (ref, hbm) in enumerate(((kg_ref, kg_hbm), (vg_ref, vg_hbm))):
-                lanes = pl.ds(h * HD, HD)
-                copies.append(pltpu.make_async_copy(ref.at[:, lanes], hbm.at[:, lanes], sems.at[m, h]))
-                copies[-1].start()
+    backs = [diagonal(back_ref, pair) for pair in range(kg_ref.shape[1] // (2 * HD))]
+    for i in range(length // ROWS):
+        here = slice(i * ROWS, (i + 1) * ROWS)
+        for pair, back in enumerate(backs):
+            lanes = slice(2 * pair * HD, 2 * (pair + 1) * HD)
+            key_pair, value_pair = mm_nt(v_ref[here, lanes], back), mm(k_ref[here, lanes], back)
+            for n in range(2):
+                h = 2 * pair + n
+                lanes, mine, rest = slice(h * HD, (h + 1) * HD), slice(n * HD, (n + 1) * HD), rests[here, h : h + 1]
+                kg_ref[here, lanes] = (kacc_ref[here, lanes].astype(F32) + rest * key_pair[:, mine]).astype(BF16)
+                vg_ref[here, lanes] = (vacc_ref[here, lanes].astype(F32) + rest * value_pair[:, mine]).astype(BF16)
+        rows = pl.ds(i * ROWS, ROWS)
+        for m, (ref, hbm) in enumerate(((kg_ref, kg_hbm), (vg_ref, vg_hbm))):
+            copies.append(pltpu.make_async_copy(ref.at[rows], hbm.at[rows], sems.at[m, i]))
+            copies[-1].start()
     for copy in copies:
         copy.wait()
 
@@ -438,7 +441,7 @@
         place, keys, values, col, back, key_part, value_part, gain_grad,
         ins=[SMEM] + [VMEM] * 7,
         out_specs=[HBM] * 3,
-        scratch=[staging] * 2 + [pltpu.VMEM(*gain_out), dma((2, heads)), dma],
+        scratch=[staging] * 2 + [pltpu.VMEM(*gain_out), dma((2, length // ROWS)), dma],
     )
     return query_grad, key_grad, value_grad, gain_grad
 

time: 114 us -> 114 us (level)
  no operation moved by 1% of the time
where the time goes in v7:
time: 114 us; the launch traced here: 113 us
  blocking collectives  79.4 us (70%)
  starting transfers between devices  15.1 us (13%)
  Pallas kernels  13.5 us (12%)
  waiting for transfers between devices  4.44 us (4%)
    all_to_all x4, blocking collectives, exchange(): lax.all_to_all(parts, 'seq', 0, 0, tiled=True, axis_index_groups=groups)  70.3 us
    all_to_all x2, starting transfers between devices, exchange(): lax.all_to_all(parts, 'seq', 0, 0, tiled=True, axis_index_groups=groups)  15.1 us
    pallas_call x10, Pallas kernels, call(): pl.pallas_call(kernel, out_shape=[jax.ShapeDtypeStruct(shape, dtype) for...  13.5 us
    all_to_all x1, blocking collectives, shards(): sums = lax.all_to_all(sums, 'tp', 0, 0, tiled=True)  9.03 us
    all_to_all x2, waiting for transfers between devices, exchange(): lax.all_to_all(parts, 'seq', 0, 0, tiled=True, axis_index_groups=groups)  4.44 us
  transfers between devices with their start and end apart: 2, of which 2 were waited for; matrix products, arithmetic and copies ran while one was open for 0% of the time, Pallas kernels for 6%

profile of v7, /device:TPU:1, one launch (start us, length us, event | category | flops | bytes accessed | tf_op | source)
XLA Modules:
  0.0 113.1 jit_solution(2501327224412361157)
XLA Ops:
  0.6 2.1 %shard_map.93 = bf16[8,72,128]{2,1,0:T(8,128)(2,1)S(1)} custom-call(s32[1]{0:T(128)} %bitcast.2.me_ref, bf16[512,512]{1,0:T(8,128)(2,1)} %k_ref.3, bf16[512,512]{1,0:T(8,128)(2,1)} %v_ref.3, f32[4,512]{1,0:T(4,128)} %bitcast.8), custom_call_target="tpu_custom_call" | custom-call | tf_op jit(solution)/shard_map/pallas_call | solution.py:353
  2.8 15.2 %all_to_all.35.got_ref = bf16[8,72,128]{2,1,0:T(8,128)(2,1)S(1)} all-to-all(bf16[8,72,128]{2,1,0:T(8,128)(2,1)S(1)} %shard_map.93), channel_id=1, replica_groups={{0,8,16,24,32,40,48,56},{64,72,80,88,96,104,112,120},{128,136,144,152,1..., dimensions={0} | all-to-all | bytes 294912 | tf_op jit(solution)/shard_map/all_to_all | solution.py:369
  18.0 27.0 %all_to_all.36.far_ref = bf16[8,72,128]{2,1,0:T(8,128)(2,1)S(1)} all-to-all(bf16[8,72,128]{2,1,0:T(8,128)(2,1)S(1)} %get-tuple-element.25), channel_id=1, replica_groups={{0,64,128,192,256,320,384,448},{8,72,136,200,264,328,392,456},{16,80,14..., dimensions={0} | all-to-all | bytes 294912 | tf_op jit(solution)/shard_map/all_to_all | solution.py:369
  45.0 0.7 shard_map.95
  45.8 0.0 copy-start.3
  45.8 7.6 %all-to-all-start.2 = ((bf16[8,64,128]{2,1,0:T(8,128)(2,1)}), bf16[8,64,128]{2,1,0:T(8,128)(2,1)S(1)}, u32[]{:S(2)}, u32[]{:S(2)}) async-start(bf16[8,64,128]{2,1,0:T(8,128)(2,1)} %get-tuple-element.27.after_ref), calls=%async_computation.2 | async-start | bytes 262144 | tf_op jit(solution)/shard_map/all_to_all | solution.py:369
  53.4 0.0 copy-done.3
  53.4 0.0 copy-start
  53.4 2.8 %shard_map.96 = (f32[512,512]{1,0:T(8,128)S(1)}, bf16[512,512]{1,0:T(8,128)(2,1)S(1)}, f32[4,512]{1,0:T(4,128)S(1)}, f32[512,8]{1,0:T(8,128)S(1)}, f32[1,512]{1,0:T(1,128)S(1)}) custom-call(bf16[512,512]{1,0:T(8,128)(2,1)} %q_hbm.3, bf16[512,512]{1,0:T(8,128)(2,1)} %k_ref.3, bf16[512,512]{1,0:T(8,128)(2,1)} %v_ref.3, f32[1,512]{1,0:T(1,128)} %bitcast.10, ...), custom_call_target="tpu_custom_call" | custom-call | flops 2000000000 | bytes 3000000 | tf_op jit(solution)/shard_map/pallas_call | solution.py:353
  56.2 3.0 %all-to-all-done.2 = bf16[8,64,128]{2,1,0:T(8,128)(2,1)S(1)} async-done(((bf16[8,64,128]{2,1,0:T(8,128)(2,1)}), bf16[8,64,128]{2,1,0:T(8,128)(2,1)S(1)}, u32[]{:S(2)}, u32[]{:S(2)}) %all-to-all-start.2) | async-done | bytes 131104 | tf_op jit(solution)/shard_map/all_to_all | solution.py:369
  59.2 0.0 copy-done
  59.2 0.5 shard_map.97
  59.7 9.0 %all_to_all.37.sums_ref = f32[8,8,128]{2,1,0:T(8,128)S(1)} all-to-all(f32[8,8,128]{2,1,0:T(8,128)S(1)} %get-tuple-element.31), channel_id=1, replica_groups=mesh['seq'=64,'tp'=8] {'tp'}, dimensions={0} | all-to-all | bytes 65536 | tf_op jit(solution)/shard_map/all_to_all | solution.py:410
  68.7 0.8 shard_map.98
  69.5 10.8 %all_to_all.38.got_ref = bf16[8,72,128]{2,1,0:T(8,128)(2,1)S(1)} all-to-all(bf16[8,72,128]{2,1,0:T(8,128)(2,1)S(1)} %get-tuple-element.36), channel_id=1, replica_groups={{0,8,16,24,32,40,48,56},{64,72,80,88,96,104,112,120},{128,136,144,152,1..., dimensions={0} | all-to-all | bytes 294912 | tf_op jit(solution)/shard_map/all_to_all | solution.py:369
  80.3 0.0 copy-start.1
  80.4 17.4 %all_to_all.39.far_ref = bf16[8,72,128]{2,1,0:T(8,128)(2,1)S(1)} all-to-all(bf16[8,72,128]{2,1,0:T(8,128)(2,1)S(1)} %shard_map.99), channel_id=1, replica_groups={{0,64,128,192,256,320,384,448},{8,72,136,200,264,328,392,456},{16,80,14..., dimensions={0} | all-to-all | bytes 294912 | tf_op jit(solution)/shard_map/all_to_all | solution.py:369
  97.7 0.7 shard_map.100
  98.4 7.5 %all-to-all-start.6 = ((bf16[8,64,128]{2,1,0:T(8,128)(2,1)}), bf16[8,64,128]{2,1,0:T(8,128)(2,1)S(1)}, u32[]{:S(2)}, u32[]{:S(2)}) async-start(bf16[8,64,128]{2,1,0:T(8,128)(2,1)} %get-tuple-element.38.after_ref), calls=%async_computation.6 | async-start | bytes 262144 | tf_op jit(solution)/shard_map/all_to_all | solution.py:369
  105.9 0.0 copy-done.1
  105.9 0.0 copy-done.2
  105.9 4.3 %shard_map.101 = (bf16[512,512]{1,0:T(8,128)(2,1)}, bf16[512,512]{1,0:T(8,128)(2,1)S(1)}, bf16[512,512]{1,0:T(8,128)(2,1)S(1)}) custom-call(bf16[512,512]{1,0:T(8,128)(2,1)} %q_hbm.3, bf16[512,512]{1,0:T(8,128)(2,1)S(1)} %copy-done.1, bf16[512,512]{1,0:T(8,128)(2,1)S(1)} %copy-done.2, bf16[512,512]{1,0:T(8,128)(2,1)S(1)} %get-tuple-element.33.grad_ref, ...), custom_call_target="tpu_custom_call" | custom-call | flops 4000000000 | bytes 5000000 | tf_op jit(solution)/shard_map/pallas_call | solution.py:353
  110.2 1.5 %all-to-all-done.6 = bf16[8,64,128]{2,1,0:T(8,128)(2,1)S(1)} async-done(((bf16[8,64,128]{2,1,0:T(8,128)(2,1)}), bf16[8,64,128]{2,1,0:T(8,128)(2,1)S(1)}, u32[]{:S(2)}, u32[]{:S(2)}) %all-to-all-start.6) | async-done | bytes 131104 | tf_op jit(solution)/shard_map/all_to_all | solution.py:369
  111.7 1.4 %shard_map.102 = (bf16[512,512]{1,0:T(8,128)(2,1)}, bf16[512,512]{1,0:T(8,128)(2,1)}, f32[8]{0:T(128)}) custom-call(s32[1]{0:T(128)} %bitcast.2.me_ref, bf16[512,512]{1,0:T(8,128)(2,1)S(1)} %copy-done.1, bf16[512,512]{1,0:T(8,128)(2,1)S(1)} %copy-done.2, f32[512,8]{1,0:T(8,128)S(1)} %get-tuple-element.35.col_ref, bf16[512,128]{1,0:T(8,128)(2,1)S(1)} %bitcast.7, ...), custom_call_target="tpu_custom_call" | custom-call | tf_op jit(solution)/shard_map/pallas_call | solution.py:353
  (3 shorter events, 0.1 us)
Async XLA Ops:
  45.8 7.6 %copy-start.3 = (f32[512,4]{0,1:T(4,128)S(1)}, f32[512,4]{0,1:T(4,128)}, u32[]{:S(2)}) copy-start(f32[512,4]{0,1:T(4,128)} %param.11) | copy-start | bytes 24580
  45.8 13.4 %all-to-all-start.2 = ((bf16[8,64,128]{2,1,0:T(8,128)(2,1)}), bf16[8,64,128]{2,1,0:T(8,128)(2,1)S(1)}, u32[]{:S(2)}, u32[]{:S(2)}) async-start(bf16[8,64,128]{2,1,0:T(8,128)(2,1)} %get-tuple-element.27.after_ref), calls=%async_computation.2 | async-start | bytes 262144 | tf_op jit(solution)/shard_map/all_to_all | solution.py:369
  53.4 5.8 %copy-start = (bf16[512,512]{1,0:T(8,128)(2,1)S(1)}, bf16[512,512]{1,0:T(8,128)(2,1)}, u32[]{:S(2)}) copy-start(bf16[512,512]{1,0:T(8,128)(2,1)} %og_ref.3) | copy-start | bytes 1572868
  80.3 25.6 %copy-start.1 = (bf16[512,512]{1,0:T(8,128)(2,1)S(1)}, bf16[512,512]{1,0:T(8,128)(2,1)}, u32[]{:S(2)}) copy-start(bf16[512,512]{1,0:T(8,128)(2,1)} %k_ref.3) | copy-start | bytes 1572868
  80.3 25.6 %copy-start.2 = (bf16[512,512]{1,0:T(8,128)(2,1)S(1)}, bf16[512,512]{1,0:T(8,128)(2,1)}, u32[]{:S(2)}) copy-start(bf16[512,512]{1,0:T(8,128)(2,1)} %v_ref.3) | copy-start | bytes 1572868
  98.4 13.3 %all-to-all-start.6 = ((bf16[8,64,128]{2,1,0:T(8,128)(2,1)}), bf16[8,64,128]{2,1,0:T(8,128)(2,1)S(1)}, u32[]{:S(2)}, u32[]{:S(2)}) async-start(bf16[8,64,128]{2,1,0:T(8,128)(2,1)} %get-tuple-element.38.after_ref), calls=%async_computation.6 | async-start | bytes 262144 | tf_op jit(solution)/shard_map/all_to_all | solution.py:369
